TPU v7x, 32 devices: a whole 2x2x4 slice. The times are simulated.
32 devices in a mesh: grp: 4 (over y, x), dev: 8 (over z, core).
Axes of the slice: x: 2, y: 2, z: 4, core: 2. Of those that a mesh axis runs over, the one named last changes fastest.
Arguments:
- adjacency: float32 [256, 1024, 128], P('dev', 'grp'), may hold values from 0.05 to 5
- features: float32 [32768, 256], P('dev', 'grp'), may hold values from -6 to 6
- col_slot: int32 [256, 128], P('dev'), may hold values from 0 to 127, each once within a row
- row_slot: int32 [8, 128], P('grp'), may hold values from 0 to 127, each once within a row
- row_pair: int32 [8], replicated, may hold values from 0 to 7, each once
- col_pair: int32 [32], replicated, may hold values from 0 to 31, each once
- col_offset: int32 [32], replicated, may hold values from 0 to 7, as said below
Outputs:
- coarse_adjacency: float32 [128, 512, 128], P('dev', 'grp')
- coarse_features: float32 [16384, 256], P('dev', 'grp')
Inputs may be any that keep to these rules, and one draw needn't show every extreme that they name: `col_offset`: each value appears at most 8 times; some value appears exactly 8 times.
All inputs are finite; a program needn't handle non-finite values.
Results may differ from a plain program's by a relative error of at most 0.00007.
Values sent between devices are 32-bit elements; how exact they have to be, the bound alone decides.
No kernel may reach another device: no remote copies, remote signals or barrier semaphores. Data moves between devices by JAX's collectives and lax.ppermute only.
A program may use at most 64 MiB of HBM per device.

v0:
```python
import jax
import jax.numpy as jnp
from jax import lax
from jax.sharding import PartitionSpec as P


def body(adjacency, features, col_slot, row_slot, row_pair, col_pair, col_offset):
    highest = lax.Precision.HIGHEST
    dev_count = lax.axis_size("dev")
    group_index = lax.axis_index("grp")
    device = lax.axis_index("dev")
    blocks, rows_here, tile_size = adjacency.shape
    row_blocks = row_slot.shape[0]
    feat_width = features.shape[1]
    capacity = 2 * blocks // dev_count
    positions = jnp.arange(blocks, dtype=jnp.int32)
    lane_ids = jnp.arange(tile_size, dtype=jnp.int32)
    feature_blocks = features.reshape(blocks, tile_size, feat_width)
    col_onehot = (col_slot[:, :, None] == lane_ids[None, None, :]).astype(jnp.float32)
    permuted = jnp.einsum("brj,bju->bru", adjacency, col_onehot, precision=highest)
    feat_perm = jnp.einsum("bju,bjf->buf", col_onehot, feature_blocks, precision=highest)
    slab_blocks = row_pair.shape[0]
    slab_ids = jnp.arange(slab_blocks, dtype=jnp.int32)
    row_place = jnp.sum(
        jnp.where(row_pair[None, :] == slab_ids[:, None], slab_ids[None, :], 0), axis=1
    )
    own_blocks = group_index * row_blocks + jnp.arange(row_blocks, dtype=jnp.int32)
    own_onehot = (own_blocks[:, None] == slab_ids[None, :]).astype(jnp.int32)
    coarse_row = jnp.sum(own_onehot * row_place[None, :], axis=1) // 2
    coarse_count = slab_blocks // 2
    row_onehot = (row_slot[:, None, :] == lane_ids[None, :, None]).astype(jnp.float32)
    block_onehot = (
        coarse_row[None, :] == jnp.arange(coarse_count, dtype=jnp.int32)[:, None]
    ).astype(jnp.float32)
    same_value = col_offset[:, None] == col_offset[None, :]
    earlier = positions[None, :] < positions[:, None]
    send_slot = jnp.sum(jnp.logical_and(same_value, earlier), axis=1)
    target_dev = (device + col_offset) % dev_count
    source = (device - col_offset) % dev_count
    slot_ids = jnp.arange(dev_count * capacity, dtype=jnp.int32)
    send_key = target_dev * capacity + send_slot
    placing = (send_key[None, :] == slot_ids[:, None]).astype(jnp.float32)
    recv_key = source * capacity + send_slot
    ordered = jnp.sum(
        jnp.where(col_pair[:, None] == positions[None, :], recv_key[None, :], 0), axis=1
    )
    picking = (ordered[:, None] == slot_ids[None, :]).astype(jnp.float32)
    merging = picking.reshape(blocks // 2, 2, dev_count * capacity).sum(axis=1)
    tile_shape = permuted.shape[1:]
    send_tiles = jnp.einsum("kp,pxy->kxy", placing, permuted, precision=highest).reshape(
        (dev_count, capacity) + tile_shape
    )
    send_feats = jnp.einsum("kp,pxy->kxy", placing, feat_perm, precision=highest).reshape(
        dev_count, capacity, tile_size, feat_width
    )
    got_tiles = lax.all_to_all(send_tiles, "dev", split_axis=0, concat_axis=0, tiled=True)
    got_feats = lax.all_to_all(send_feats, "dev", split_axis=0, concat_axis=0, tiled=True)
    flat_tiles = got_tiles.reshape((dev_count * capacity,) + tile_shape)
    flat_feats = got_feats.reshape(dev_count * capacity, tile_size, feat_width)
    merged_tiles = jnp.einsum("km,mxy->kxy", merging, flat_tiles, precision=highest)
    merged_feats = jnp.einsum("km,mxy->kxy", merging, flat_feats, precision=highest)
    count = merged_tiles.shape[0]
    split_rows = merged_tiles.reshape(count, row_blocks, tile_size, tile_size)
    reordered = jnp.einsum("rui,brij->bruj", row_onehot, split_rows, precision=highest)
    placed = jnp.einsum("cr,bruj->bcuj", block_onehot, reordered, precision=highest)
    coarse_adjacency = lax.psum_scatter(
        placed.reshape(count, coarse_count * tile_size, tile_size),
        "grp",
        scatter_dimension=1,
        tiled=True,
    )
    return (coarse_adjacency, merged_feats.reshape(-1, feat_width))


def solution(mesh):
    in_specs = (
        P("dev", "grp", None),
        P("dev", "grp"),
        P("dev", None),
        P("grp", None),
        P(),
        P(),
        P(),
    )
    out_specs = (P("dev", "grp", None), P("dev", "grp"))
    return jax.shard_map(body, mesh=mesh, in_specs=in_specs, out_specs=out_specs, check_vma=False)
```

profile of v0, /device:TPU:0, one launch (start us, length us, event | category | flops | bytes accessed | tf_op | source)
XLA Modules:
  0.0 311.6 jit_solution(3873266592628237912)
XLA Ops:
  7.2 0.0 copy-start
  7.2 0.9 convert_reduce_fusion.1
  8.1 5.8 %convolution_bitcast_fusion.2 = f32[32,256,128]{1,2,0:T(8,128)} fusion(f32[32,256,128]{2,1,0:T(8,128)} %param.7, s32[32,128]{1,0:T(8,128)} %param.9), kind=kOutput, calls=%fused_computation.2 | convolution fusion | flops 1611661312 | bytes 8404992 | tf_op jit(solution)/shard_map/brj,bju->bru/dot_general | solution.py:20
  13.9 5.5 %copy.34 = f32[32,256,128]{2,0,1:T(8,128)} copy(f32[32,256,128]{1,2,0:T(8,128)} %convolution_bitcast_fusion.2) | data formatting | bytes 8388608 | tf_op jit(solution)/shard_map/brj,bju->bru/dot_general | solution.py:20
  19.4 0.0 copy-done.3
  19.4 5.5 %convolution_bitcast_fusion = f32[8,8,256,128]{3,1,0,2:T(8,128)S(1)} fusion(f32[32,256,128]{2,0,1:T(8,128)} %copy.34, s32[32]{0:T(128)S(1)} %get-tuple-element.3), kind=kOutput, calls=%fused_computation | convolution fusion | flops 805308416 | bytes 12583040 | tf_op jit(solution)/shard_map/kp,pxy->kxy/dot_general | solution.py:50
  25.0 3.8 %copy.35 = f32[8,8,256,128]{3,1,2,0:T(8,128)} copy(f32[8,8,256,128]{3,1,0,2:T(8,128)S(1)} %convolution_bitcast_fusion) | data formatting | bytes 16777216 | tf_op jit(solution)/shard_map/reshape | solution.py:50
  28.7 6.5 %all-to-all-start = ((f32[8,8,256,128]{3,1,2,0:T(8,128)}), f32[8,8,256,128]{3,1,2,0:T(8,128)}, u32[]{:S(2)}, u32[]{:S(2)}) async-start(f32[8,8,256,128]{3,1,2,0:T(8,128)} %copy.35), calls=%async_computation | async-start | bytes 16777216 | tf_op jit(solution)/shard_map/all_to_all | solution.py:56
  35.2 0.2 reduce-scatter.2.cloned.1.call-start
  35.4 0.2 select_reduce_fusion
  35.6 0.1 eq.132
  35.7 0.1 copy.32
  35.8 0.1 select_reduce_fusion.1
  35.9 0.1 convert_reduce_fusion
  36.0 0.2 fusion.30
  36.2 183.0 %all-to-all-done = f32[8,8,256,128]{3,1,2,0:T(8,128)} async-done(((f32[8,8,256,128]{3,1,2,0:T(8,128)}), f32[8,8,256,128]{3,1,2,0:T(8,128)}, u32[]{:S(2)}, u32[]{:S(2)}) %all-to-all-start) | async-done | bytes 8388640 | tf_op jit(solution)/shard_map/all_to_all | solution.py:56
  219.2 4.9 %copy.36 = f32[8,8,256,128]{3,2,1,0:T(8,128)S(1)} copy(f32[8,8,256,128]{3,1,2,0:T(8,128)} %all-to-all-done) | data formatting | bytes 16777216 | tf_op jit(solution)/shard_map/all_to_all | solution.py:56
  224.1 4.9 %copy.37 = f32[256,128,64]{1,2,0:T(8,128)S(1)} copy(f32[256,128,64]{1,0,2:T(8,128)S(1)} %bitcast.57) | data formatting | bytes 16777216 | tf_op jit(solution)/shard_map/km,mxy->kxy/dot_general | solution.py:60
  228.9 0.0 copy-start.2
  228.9 4.1 %fusion.23 = f32[16,2,128,128]{3,0,2,1:T(8,128)S(1)} fusion(f32[2,128,128,64]{2,3,1,0:T(8,128)S(1)} %bitcast.58, f32[16,64]{1,0:T(8,128)S(1)} %convert_reduce_fusion), kind=kOutput, calls=%fused_computation.31 | convolution fusion | flops 402653184 | bytes 10489856 | tf_op jit(solution)/shard_map/km,mxy->kxy/dot_general | solution.py:60
  233.0 3.6 %fusion.7 = f32[16,2,128,128]{2,3,0,1:T(8,128)} fusion(f32[16,2,128,128]{3,0,2,1:T(8,128)S(1)} %fusion.23, s32[2,128]{1,0:T(2,128)S(1)} %copy-done.2), kind=kOutput, calls=%fused_computation.11 | convolution fusion | flops 805339136 | bytes 4195328 | tf_op jit(solution)/shard_map/rui,brij->bruj/dot_general | solution.py:64
  236.6 2.9 copy.39
  239.6 4.5 %convolution_bitcast_fusion.1 = f32[16,4,128,128]{3,1,2,0:T(4,128)S(1)} fusion(f32[16,2,128,128]{3,1,2,0:T(2,128)S(1)} %copy.39, s32[2]{0:T(128)S(1)} %and_select_fusion), kind=kOutput, calls=%fused_computation.1 | convolution fusion | flops 25165832 | bytes 6291464 | tf_op jit(solution)/shard_map/cr,bruj->bcuj/dot_general | solution.py:65
  244.1 2.5 copy.40
  246.6 0.0 reduce-scatter.2.cloned.1.call-update
  246.7 0.7 copy-done.1
  247.4 2.0 fusion.5
  249.4 1.7 convolution_bitcast_fusion.3
  251.1 0.1 copy.43
  251.2 51.5 %all_to_all.10 = f32[8,8,128,64]{2,1,3,0:T(8,128)S(1)} all-to-all(f32[8,8,128,64]{2,1,3,0:T(8,128)S(1)} %copy.43), channel_id=1, replica_groups=mesh['grp'=4,'dev'=8] {'dev'}, dimensions={0} | all-to-all | bytes 4194304 | tf_op jit(solution)/shard_map/all_to_all | solution.py:57
  302.7 1.1 fusion
  303.8 1.0 copy.66
  (12 shorter events, 0.0 us)
Async XLA Ops:
  7.2 239.5 %copy-start = (f32[4096,64]{0,1:T(8,128)S(1)}, f32[4096,64]{0,1:T(8,128)}, u32[]{:S(2)}) copy-start(f32[4096,64]{0,1:T(8,128)} %param.8) | copy-start | bytes 3145732
  13.9 5.5 %copy-start.3 = (s32[32]{0:T(128)S(1)}, s32[32]{0:T(128)}, u32[]{:S(2)}) copy-start(s32[32]{0:T(128)} %param.13) | copy-start | bytes 388
  28.7 6.7 %copy-start.4 = (s32[32]{0:T(128)S(1)}, s32[32]{0:T(128)}, u32[]{:S(2)}) copy-start(s32[32]{0:T(128)} %param.12) | copy-start | bytes 388
  28.7 7.0 %copy-start.5 = (s32[8]{0:T(128)S(1)}, s32[8]{0:T(128)}, u32[]{:S(2)}) copy-start(s32[8]{0:T(128)} %param.11) | copy-start | bytes 100
  28.7 190.5 %all-to-all-start = ((f32[8,8,256,128]{3,1,2,0:T(8,128)}), f32[8,8,256,128]{3,1,2,0:T(8,128)}, u32[]{:S(2)}, u32[]{:S(2)}) async-start(f32[8,8,256,128]{3,1,2,0:T(8,128)} %copy.35), calls=%async_computation | async-start | bytes 16777216 | tf_op jit(solution)/shard_map/all_to_all | solution.py:56
  35.2 269.6 %reduce-scatter.2.cloned.1.call-start = ((), (), s32[]{:S(2)}) async-start(), calls=%async_computation.3 | async-start | bytes 5242880 | tf_op jit(solution)/shard_map/reduce_scatter | solution.py:66
  228.9 4.1 %copy-start.2 = (s32[2,128]{1,0:T(2,128)S(1)}, s32[2,128]{1,0:T(2,128)}, u32[]{:S(2)}) copy-start(s32[2,128]{1,0:T(2,128)} %param.10) | copy-start | bytes 3076
  246.6 0.7 copy-start.1
Sparse Core Ops, SparseCore 0:
  246.8 51.5 reduce-scatter.1
where the time goes:
time: 312 us
  waiting for transfers between devices  183 us (59%)
  blocking collectives  51.5 us (17%)
  matrix products  28.4 us (9%)
  local copies, waits for them, and re-layouts  26.4 us (8%)
  between operations  14.2 us (5%)
  starting transfers between devices  6.67 us (2%)
    all_to_all x1, waiting for transfers between devices, body(): lax.all_to_all(send_tiles, 'dev', split_axis=0, concat_axis=0, tiled=True)  183 us
    all_to_all x1, blocking collectives, body(): lax.all_to_all(send_feats, 'dev', split_axis=0, concat_axis=0, tiled=True)  51.5 us
    all_to_all x1, starting transfers between devices, body(): lax.all_to_all(send_tiles, 'dev', split_axis=0, concat_axis=0, tiled=True)  6.45 us
  transfers between devices with their start and end apart: 2, of which 1 were waited for; matrix products, arithmetic and copies ran while one was open for 2% of the time, Pallas kernels for 0%

commit v1 on v0

v1 whole, which is shorter than its diff:
```python
import functools
import jax
import jax.numpy as jnp
from jax import lax
from jax.experimental import pallas as pl
from jax.experimental.pallas import tpu as pltpu
from jax.sharding import PartitionSpec as P

TILE = 128
GROUPS = 4
ANY = pl.BlockSpec(memory_space=pl.ANY)
VMEM = pl.BlockSpec(memory_space=pltpu.VMEM)
SMEM = pl.BlockSpec(memory_space=pltpu.SMEM)


def split16(x):
    high = x.astype(jnp.bfloat16)
    low = (x - high.astype(jnp.float32)).astype(jnp.bfloat16)
    return high, low


def rows_kernel(first, rows, step_blocks, pair_ref, slot_ref, *refs):
    tiles = refs[: 2 * step_blocks]
    send_x, keep_x, send_y, keep_y, onehot = refs[2 * step_blocks :]

    @pl.when(pl.program_id(0) == 0)
    def _():
        group = lax.axis_index("grp")
        keys = []
        for r in range(2):
            owner = jnp.int32(0)
            for h in range(2 * GROUPS):
                owner = jnp.where(pair_ref[h] == 2 * group + r, h // 2, owner)
            away = jnp.bitwise_xor(owner, group)
            local = slot_ref[r : r + 1, :] - first
            inside = jnp.logical_and(local >= 0, local < rows)
            keys.append(jnp.where(inside, away * rows + local, -1))
        key = jnp.concatenate(keys + keys, axis=1)
        place = lax.broadcasted_iota(jnp.int32, (GROUPS * rows, 4 * TILE), 0)
        onehot[...] = (place == key).astype(jnp.float32).astype(jnp.bfloat16)

    def mapped(pair):
        x = jnp.concatenate([tile[0] for tile in pair], axis=1)
        high, low = split16(x)
        both = jnp.concatenate([high, low], axis=0)
        return jnp.dot(onehot[...], both, preferred_element_type=jnp.float32)

    for i in range(0, step_blocks, 2):
        full = mapped(tiles[i : i + 2])
        for j in range(2):
            lanes = slice(j * TILE, (j + 1) * TILE)
            part = [full[m * rows : (m + 1) * rows, lanes] for m in range(GROUPS)]
            keep_x[0, i + j], send_x[0, i + j], keep_x[1, i + j], send_x[1, i + j] = part
        full = mapped(tiles[step_blocks + i : step_blocks + i + 2])
        for j in range(2):
            lanes = slice(j * TILE, (j + 1) * TILE)
            part = [full[m * rows : (m + 1) * rows, lanes] for m in range(GROUPS)]
            keep_y[0, i + j], keep_y[1, i + j], send_y[0, i + j], send_y[1, i + j] = part


def row_map(adjacency, row_slot, row_pair, first, rows):
    blocks, own_rows, tile = adjacency.shape
    half = blocks // 2
    step_blocks = 4
    steps = half // step_blocks

    def at(base, j):
        return pl.BlockSpec((1, own_rows, tile), lambda i: (base + step_blocks * i + j, 0, 0))

    out = jax.ShapeDtypeStruct((2, half, rows, tile), jnp.float32)
    return pl.pallas_call(
        functools.partial(rows_kernel, first, rows, step_blocks),
        grid=(steps,),
        out_shape=[out] * 4,
        in_specs=[SMEM, VMEM]
        + [at(0, j) for j in range(step_blocks)]
        + [at(half, j) for j in range(step_blocks)],
        out_specs=[pl.BlockSpec((2, step_blocks, rows, tile), lambda i: (0, i, 0, 0))] * 4,
        scratch_shapes=[pltpu.VMEM((GROUPS * rows, 4 * tile), jnp.bfloat16)],
        compiler_params=pltpu.CompilerParams(vmem_limit_bytes=32 << 20),
        cost_estimate=pl.CostEstimate(flops=int(2e9), bytes_accessed=12 << 20, transcendentals=0),
        name="row_map",
    )(row_pair, row_slot, *([adjacency] * (2 * step_blocks)))


def lanes_of(x, slots):
    place = lax.broadcasted_iota(jnp.int32, (TILE, TILE), 0)
    onehot = (place == slots).astype(jnp.float32).astype(jnp.bfloat16)
    high, low = split16(x)
    both = lax.dot_general(
        jnp.concatenate([high, low], axis=0),
        onehot,
        (((1,), (1,)), ((), ())),
        preferred_element_type=jnp.float32,
    )
    return both[: x.shape[0]] + both[x.shape[0] :]


def features_kernel(blocks, slot_ref, col_ref, x_ref, out_ref):
    for p in range(blocks):
        lanes = slice(p * TILE, (p + 1) * TILE)
        out_ref[slot_ref[p]] = lanes_of(x_ref[:, lanes], col_ref[p : p + 1, :])
    for p in range(blocks, out_ref.shape[0]):
        out_ref[p] = jnp.zeros(out_ref.shape[1:], jnp.float32)


def columns_kernel(step_blocks, steps, slot_ref, col_ref, *refs):
    ins, out_ref = refs[:6], refs[6]
    i = pl.program_id(0)
    for half in range(2):
        keep, got1, got2 = ins[3 * half : 3 * half + 3]
        for j in range(step_blocks):
            p = half * steps * step_blocks + i * step_blocks + j
            x = keep[0, j] + got1[0, j] + got2[j]
            out_ref[slot_ref[p]] = lanes_of(x, col_ref[pl.ds(p, 1), :])

    @pl.when(i == 0)
    def _():
        for p in range(2 * steps * step_blocks, out_ref.shape[0]):
            out_ref[p] = jnp.zeros(out_ref.shape[1:], jnp.float32)


def column_map(keep_x, got1_x, got2_x, keep_y, got1_y, got2_y, col_slot, slot, pad):
    half, rows, tile = got2_x.shape
    step_blocks = 4
    steps = half // step_blocks
    four = pl.BlockSpec((1, step_blocks, rows, tile), lambda i: (0, i, 0, 0))
    three = pl.BlockSpec((step_blocks, rows, tile), lambda i: (i, 0, 0))
    shape = (2 * half + pad, rows, tile)
    return pl.pallas_call(
        functools.partial(columns_kernel, step_blocks, steps),
        grid=(steps,),
        out_shape=jax.ShapeDtypeStruct(shape, jnp.float32),
        in_specs=[SMEM, VMEM] + [four, four, three] * 2,
        out_specs=pl.BlockSpec(shape, lambda i: (0, 0, 0)),
        compiler_params=pltpu.CompilerParams(vmem_limit_bytes=32 << 20),
        cost_estimate=pl.CostEstimate(flops=int(1e9), bytes_accessed=4 << 20, transcendentals=0),
        name="column_map",
    )(slot, col_slot, keep_x, got1_x, got2_x, keep_y, got1_y, got2_y)


def feature_map(features_t, col_slot, slot, pad):
    width, columns = features_t.shape
    blocks = columns // TILE
    return pl.pallas_call(
        functools.partial(features_kernel, blocks),
        out_shape=jax.ShapeDtypeStruct((blocks + pad, width, TILE), jnp.float32),
        in_specs=[SMEM, VMEM, VMEM],
        out_specs=VMEM,
        compiler_params=pltpu.CompilerParams(vmem_limit_bytes=32 << 20),
        cost_estimate=pl.CostEstimate(flops=int(1e9), bytes_accessed=2 << 20, transcendentals=0),
        name="feature_map",
    )(slot, col_slot, features_t)


def merge_kernel(sizes, in_lanes, src_ref, *refs):
    pieces = refs[: len(sizes)]
    out_ref, held, sem = refs[-3:]
    copies = []
    at = 0
    for n, (piece, size) in enumerate(zip(pieces, sizes)):
        copies.append(
            pltpu.make_async_copy(piece.at[pl.ds(0, size)], held.at[pl.ds(at, size)], sem.at[n])
        )
        at += size
    for copy in copies:
        copy.start()
    for copy in copies:
        copy.wait()
    count = src_ref.shape[0] // 2
    for k in range(count):
        total = held[src_ref[2 * k]] + held[src_ref[2 * k + 1]]
        if in_lanes:
            out_ref[:, k * TILE : (k + 1) * TILE] = total
        else:
            out_ref[k] = total


def merge_features(pieces, sizes, src):
    width = pieces[0].shape[1]
    count = src.shape[0] // 2
    return pl.pallas_call(
        functools.partial(merge_kernel, sizes, True),
        out_shape=jax.ShapeDtypeStruct((width, count * TILE), jnp.float32),
        in_specs=[SMEM] + [ANY] * len(pieces),
        out_specs=VMEM,
        scratch_shapes=[
            pltpu.VMEM((sum(sizes), width, TILE), jnp.float32),
            pltpu.SemaphoreType.DMA((len(pieces),)),
        ],
        compiler_params=pltpu.CompilerParams(vmem_limit_bytes=32 << 20),
        cost_estimate=pl.CostEstimate(flops=int(1e6), bytes_accessed=3 << 20, transcendentals=0),
        name="merge_features",
    )(src, *pieces)


def merge_tiles(pieces, sizes, src, first, before):
    rows = pieces[0].shape[1]
    count = src.shape[0] // 2
    operands = (src, *pieces) + (() if before is None else (before,))
    return pl.pallas_call(
        functools.partial(merge_kernel, sizes, False),
        grid=(1,),
        out_shape=jax.ShapeDtypeStruct((count, TILE, TILE), jnp.float32),
        in_specs=[SMEM] + [ANY] * (len(operands) - 1),
        out_specs=pl.BlockSpec((count, rows, TILE), lambda i: (0, first // rows, 0)),
        input_output_aliases={} if before is None else {len(operands) - 1: 0},
        scratch_shapes=[
            pltpu.VMEM((sum(sizes), rows, TILE), jnp.float32),
            pltpu.SemaphoreType.DMA((len(pieces),)),
        ],
        compiler_params=pltpu.CompilerParams(vmem_limit_bytes=32 << 20),
        cost_estimate=pl.CostEstimate(flops=int(1e6), bytes_accessed=3 << 20, transcendentals=0),
        name="merge_tiles",
    )(*operands)


def turn(x, shift, dev_count):
    return lax.ppermute(x, "dev", [(i, (i + shift) % dev_count) for i in range(dev_count)])


def exchange_some(sorted_blocks, counts, starts, capacity, dev_count):
    unit = capacity // 2
    rest = sorted_blocks.shape[1:]

    def branch(shift, units):
        def run(blocks, start):
            if units == 0:
                return jnp.zeros((capacity,) + rest, jnp.float32)
            size = units * unit
            piece = lax.dynamic_slice(blocks, (start, 0, 0), (size,) + rest)
            got = turn(piece, shift, dev_count)
            if size < capacity:
                got = jnp.concatenate([got, jnp.zeros((capacity - size,) + rest, jnp.float32)])
            return got

        return run

    pieces = [sorted_blocks]
    for shift in range(1, dev_count):
        units = (counts[shift] + unit - 1) // unit
        pieces.append(
            lax.switch(units, [branch(shift, u) for u in range(3)], sorted_blocks, starts[shift])
        )
    return pieces, [capacity] * dev_count


def exchange_all(sorted_blocks, counts, starts, capacity, dev_count):
    me = lax.axis_index("dev")
    ids = jnp.arange(dev_count * capacity, dtype=jnp.int32)
    shift = (ids // capacity - me) % dev_count
    send = jnp.take(sorted_blocks, jnp.take(starts, shift) + ids % capacity, axis=0)
    got = lax.all_to_all(send, "dev", split_axis=0, concat_axis=0, tiled=True)
    source = (me - ids // capacity) % dev_count
    return [jnp.take(got, source * capacity + ids % capacity, axis=0)], [dev_count * capacity]


def body(adjacency, features, col_slot, row_slot, row_pair, col_pair, col_offset):
    dev_count = lax.axis_size("dev")
    blocks = adjacency.shape[0]
    half = blocks // 2
    capacity = 2 * blocks // dev_count
    exchange = exchange_some if dev_count == 8 else exchange_all

    positions = jnp.arange(blocks, dtype=jnp.int32)
    same = col_offset[:, None] == col_offset[None, :]
    earlier = positions[None, :] < positions[:, None]
    rank = jnp.sum(jnp.logical_and(same, earlier).astype(jnp.int32), axis=1)
    lower = (col_offset[None, :] < col_offset[:, None]).astype(jnp.int32)
    slot = rank + jnp.sum(lower, axis=1)
    offsets = jnp.arange(dev_count, dtype=jnp.int32)
    counts = jnp.sum((col_offset[None, :] == offsets[:, None]).astype(jnp.int32), axis=1)
    starts = jnp.sum((col_offset[None, :] < offsets[:, None]).astype(jnp.int32), axis=1)
    chosen = col_pair[:, None] == positions[None, :]
    src = jnp.sum(jnp.where(chosen, (col_offset * capacity + rank)[None, :], 0), axis=1)

    x_side = [(g, g ^ 1) for g in range(GROUPS)]
    y_side = [(g, g ^ 2) for g in range(GROUPS)]

    feature_blocks = feature_map(features.T, col_slot, slot, capacity)
    pieces, sizes = exchange(feature_blocks, counts, starts, capacity, dev_count)
    coarse_features = merge_features(pieces, sizes, src).T

    coarse_adjacency = None
    rows = TILE // 2
    for first in range(0, TILE, rows):
        send_x, keep_x, send_y, keep_y = row_map(adjacency, row_slot, row_pair, first, rows)
        got1_x = lax.ppermute(send_x, "grp", x_side)
        got1_y = lax.ppermute(send_y, "grp", y_side)
        got2_x = lax.ppermute(keep_x[1] + got1_x[1], "grp", y_side)
        got2_y = lax.ppermute(keep_y[1] + got1_y[1], "grp", x_side)
        tiles = column_map(
            keep_x, got1_x, got2_x, keep_y, got1_y, got2_y, col_slot, slot, capacity
        )
        pieces, sizes = exchange(tiles, counts, starts, capacity, dev_count)
        coarse_adjacency = merge_tiles(pieces, sizes, src, first, coarse_adjacency)
    return coarse_adjacency, coarse_features


def solution(mesh):
    in_specs = (
        P("dev", "grp", None),
        P("dev", "grp"),
        P("dev", None),
        P("grp", None),
        P(),
        P(),
        P(),
    )
    out_specs = (P("dev", "grp", None), P("dev", "grp"))
    return jax.shard_map(body, mesh=mesh, in_specs=in_specs, out_specs=out_specs, check_vma=False)
```

time: 312 us -> 238 us (0.76)
  waiting for transfers between devices: 183 us -> 129 us
  blocking collectives: 51.5 us -> 0 us
  loops' own time: 0 us -> 28.5 us
  matrix products: 28.4 us -> 0 us
  Pallas kernels: 0 us -> 27.1 us
  starting transfers between devices: 6.67 us -> 16.4 us
  between operations: 14.2 us -> 5.32 us
  other arithmetic: 1.52 us -> 7.29 us
    all_to_all x1 -> x0, waiting for transfers between devices: 183 us -> none  [body(): lax.all_to_all(send_tiles, 'dev', split_axis=0, concat_axis=0, tiled=True)]
    ppermute x0 -> x23, waiting for transfers between devices: none -> 129 us  [the longest x15 99 us: turn(): lax.ppermute(x, 'dev', [(i, (i + shift) % dev_count) for i in range(dev_c...]
    all_to_all x1 -> x0, blocking collectives: 51.5 us -> none  [body(): lax.all_to_all(send_feats, 'dev', split_axis=0, concat_axis=0, tiled=True)]
    another operation x0 -> x21, loops' own time: none -> 28.5 us  [exchange_some(): lax.switch(units, [branch(shift, u) for u in range(3)], sorted_blocks, st...]
    dot_general x8 -> x0, matrix products: 28.4 us -> none  [the longest x1 5.79 us: body(): jnp.einsum('brj,bju->bru', adjacency, col_onehot, precision=highest)]
    pallas_call x0 -> x8, Pallas kernels: none -> 27.1 us  [the longest x2 8.43 us: column_map(): pl.pallas_call(functools.partial(columns_kernel, step_blocks, steps), gri...]
    ppermute x0 -> x23, starting transfers between devices: none -> 16.4 us  [the longest x15 5.73 us: turn(): lax.ppermute(x, 'dev', [(i, (i + shift) % dev_count) for i in range(dev_c...]
    dot_general x2 -> x0, local copies, waits for them, and re-layouts: 10.4 us -> none  [the longest x1 5.5 us: body(): jnp.einsum('brj,bju->bru', adjacency, col_onehot, precision=highest)]
  transfers between devices with their start and end apart: 2 -> 23, of which waited for: 1 -> 17; matrix products, arithmetic and copies ran while one was open for 2% -> 7% of each run, Pallas kernels for 0% -> 6%
where the time goes in v1:
time: 238 us; the launch traced here: 237 us
  waiting for transfers between devices  129 us (54%)
  loops' own time  28.5 us (12%)
  Pallas kernels  27.1 us (11%)
  local copies, waits for them, and re-layouts  23.6 us (10%)
  starting transfers between devices  16.4 us (7%)
  other arithmetic  7.29 us (3%)
  between operations  5.32 us (2%)
    ppermute x15, waiting for transfers between devices, turn(): lax.ppermute(x, 'dev', [(i, (i + shift) % dev_count) for i in range(dev_c...  99 us
    another operation x21, loops' own time, exchange_some(): lax.switch(units, [branch(shift, u) for u in range(3)], sorted_blocks, st...  28.5 us
    ppermute x2, waiting for transfers between devices, body(): got1_y = lax.ppermute(send_y, 'grp', y_side)  16.9 us
    ppermute x2, waiting for transfers between devices, body(): got1_x = lax.ppermute(send_x, 'grp', x_side)  12.8 us
    dynamic_slice x15, local copies, waits for them, and re-layouts, run(): piece = lax.dynamic_slice(blocks, (start, 0, 0), (size,) + rest)  9.61 us
    pallas_call x2, Pallas kernels, column_map(): pl.pallas_call(functools.partial(columns_kernel, step_blocks, steps), gri...  8.43 us
    pallas_call x2, Pallas kernels, row_map(): pl.pallas_call(functools.partial(rows_kernel, first, rows, step_blocks),...  7.4 us
    pallas_call x2, Pallas kernels, merge_tiles(): pl.pallas_call(functools.partial(merge_kernel, sizes, False), grid=(1,),...  5.8 us
  transfers between devices with their start and end apart: 23, of which 17 were waited for; matrix products, arithmetic and copies ran while one was open for 7% of the time, Pallas kernels for 6%

profile of v1, /device:TPU:0, one launch (start us, length us, event | category | flops | bytes accessed | tf_op | source)
XLA Modules:
  0.0 237.0 jit_solution(6552021890393980020)
XLA Ops:
  4.2 3.7 %row_map.3 = (f32[2,16,64,128]{3,2,1,0:T(8,128)}, f32[2,16,64,128]{3,2,1,0:T(8,128)S(1)}, f32[2,16,64,128]{3,2,1,0:T(8,128)}, f32[2,16,64,128]{3,2,1,0:T(8,128)S(1)}) custom-call(s32[8]{0:T(128)S(1)} %copy-done.8, s32[2,128]{1,0:T(2,128)S(1)} %copy-done.7, f32[32,256,128]{2,1,0:T(8,128)S(1)} %copy-done, f32[32,256,128]{2,1,0:T(8,128)S(1)} %copy-done, ...), custom_call_target="tpu_custom_call" | custom-call | flops 2000000000 | bytes 12582912 | tf_op jit(solution)/shard_map/row_map/pallas_call | solution.py:71
  13.3 3.7 %row_map.2 = (f32[2,16,64,128]{3,2,1,0:T(8,128)}, f32[2,16,64,128]{3,2,1,0:T(8,128)S(1)}, f32[2,16,64,128]{3,2,1,0:T(8,128)}, f32[2,16,64,128]{3,2,1,0:T(8,128)S(1)}) custom-call(s32[8]{0:T(128)S(1)} %copy-done.8, s32[2,128]{1,0:T(2,128)S(1)} %copy-done.7, f32[32,256,128]{2,1,0:T(8,128)S(1)} %copy-done, f32[32,256,128]{2,1,0:T(8,128)S(1)} %copy-done, ...), custom_call_target="tpu_custom_call" | custom-call | flops 2000000000 | bytes 12582912 | tf_op jit(solution)/shard_map/row_map/pallas_call | solution.py:71
  23.3 12.8 %collective-permute-done.46.refs_1_ = f32[2,16,64,128]{3,2,1,0:T(8,128)} collective-permute-done((f32[2,16,64,128]{3,2,1,0:T(8,128)}, f32[2,16,64,128]{3,2,1,0:T(8,128)}, u32[]{:S(2)}, u32[]{:S(2)}) %collective-permute-start.46) | collective-permute-done | bytes 1048608 | tf_op jit(solution)/shard_map/ppermute | solution.py:288
  43.7 16.9 %collective-permute-done.44.refs_4_ = f32[2,16,64,128]{3,2,1,0:T(8,128)S(1)} collective-permute-done((f32[2,16,64,128]{3,2,1,0:T(8,128)}, f32[2,16,64,128]{3,2,1,0:T(8,128)S(1)}, u32[]{:S(2)}, u32[]{:S(2)}) %collective-permute-start.44) | collective-permute-done | bytes 1048608 | tf_op jit(solution)/shard_map/ppermute | solution.py:289
  67.9 10.4 %conditional.35 = (f32[8,64,128]{2,1,0:T(8,128)}) conditional(s32[]{:T(128)} %clamp.14, () %tuple.225, (s32[]{:T(128)}, f32[40,64,128]{2,1,0:T(8,128)}) %tuple.226, (s32[]{:T(128)}, f32[40,64,128]{2,1,0:T(8,128)}) %tuple.226), branch_computations={%region_47.48_spmd, %region_48.49_spmd, %region_49.50_spmd} | conditional | flops 3 | bytes 1572950 | solution.py:243
  70.7 7.7 %collective-permute-done.29 = f32[8,64,128]{2,1,0:T(8,128)} collective-permute-done((f32[8,64,128]{2,1,0:T(8,128)S(1)}, f32[8,64,128]{2,1,0:T(8,128)}, u32[]{:S(2)}, u32[]{:S(2)}) %collective-permute-start.29) | collective-permute-done | bytes 262176 | tf_op jit(solution)/shard_map/cond/branch_2_fun/ppermute | solution.py:219
  78.4 11.2 %conditional.36 = (f32[8,64,128]{2,1,0:T(8,128)}) conditional(s32[]{:T(128)} %clamp.15, () %tuple.227, (s32[]{:T(128)}, f32[40,64,128]{2,1,0:T(8,128)}) %tuple.228, (s32[]{:T(128)}, f32[40,64,128]{2,1,0:T(8,128)}) %tuple.228), branch_computations={%region_50.51_spmd, %region_51.52_spmd, %region_52.53_spmd} | conditional | flops 3 | bytes 1572950 | solution.py:243
  81.3 8.3 %collective-permute-done.31 = f32[8,64,128]{2,1,0:T(8,128)} collective-permute-done((f32[8,64,128]{2,1,0:T(8,128)S(1)}, f32[8,64,128]{2,1,0:T(8,128)}, u32[]{:S(2)}, u32[]{:S(2)}) %collective-permute-start.31) | collective-permute-done | bytes 262176 | tf_op jit(solution)/shard_map/cond/branch_2_fun/ppermute | solution.py:219
  89.6 13.0 %conditional.37 = (f32[8,64,128]{2,1,0:T(8,128)}) conditional(s32[]{:T(128)} %clamp.16, () %tuple.229, (s32[]{:T(128)}, f32[40,64,128]{2,1,0:T(8,128)}) %tuple.230, (s32[]{:T(128)}, f32[40,64,128]{2,1,0:T(8,128)}) %tuple.230), branch_computations={%region_53.54_spmd, %region_54.55_spmd, %region_55.56_spmd} | conditional | flops 3 | bytes 1572950 | solution.py:243
  92.5 10.1 %collective-permute-done.33 = f32[8,64,128]{2,1,0:T(8,128)} collective-permute-done((f32[8,64,128]{2,1,0:T(8,128)S(1)}, f32[8,64,128]{2,1,0:T(8,128)}, u32[]{:S(2)}, u32[]{:S(2)}) %collective-permute-start.33) | collective-permute-done | bytes 262176 | tf_op jit(solution)/shard_map/cond/branch_2_fun/ppermute | solution.py:219
  104.0 8.5 %conditional.40 = (f32[8,64,128]{2,1,0:T(8,128)}) conditional(s32[]{:T(128)} %clamp.19, () %tuple.235, (s32[]{:T(128)}, f32[40,64,128]{2,1,0:T(8,128)}) %tuple.236, (s32[]{:T(128)}, f32[40,64,128]{2,1,0:T(8,128)}) %tuple.236), branch_computations={%region_62.63_spmd, %region_63.64_spmd, %region_64.65_spmd} | conditional | flops 3 | bytes 1572950 | solution.py:243
  108.1 3.7 %collective-permute-done.38 = f32[4,64,128]{2,1,0:T(8,128)S(1)} collective-permute-done((f32[4,64,128]{2,1,0:T(8,128)S(1)}, f32[4,64,128]{2,1,0:T(8,128)S(1)}, u32[]{:S(2)}, u32[]{:S(2)}) %collective-permute-start.38) | collective-permute-done | bytes 131104 | tf_op jit(solution)/shard_map/cond/branch_1_fun/ppermute | solution.py:219
  112.5 6.3 %conditional.41 = (f32[8,64,128]{2,1,0:T(8,128)}) conditional(s32[]{:T(128)} %clamp.20, () %tuple.237, (s32[]{:T(128)}, f32[40,64,128]{2,1,0:T(8,128)}) %tuple.238, (s32[]{:T(128)}, f32[40,64,128]{2,1,0:T(8,128)}) %tuple.238), branch_computations={%region_65.66_spmd, %region_66.67_spmd, %region_67.68_spmd} | conditional | flops 3 | bytes 1572950 | solution.py:243
  122.1 4.3 %column_map.3.refs_0_ = f32[40,64,128]{2,1,0:T(8,128)} custom-call(s32[32]{0:T(128)S(1)} %get-tuple-element.372.slot_ref, s32[32,128]{1,0:T(8,128)S(1)} %copy-done.6, f32[2,16,64,128]{3,2,1,0:T(8,128)S(1)} %copy-done.2, f32[2,16,64,128]{3,2,1,0:T(8,128)} %collective-permute-done.46.refs_1_, f32[16,64,128]{2,1,0:T(8,128)} %collective-permute-done.47.refs_2_, ...), custom_call_target="tpu_custom_call" | custom-call | flops 1000000000 | bytes 4194304 | tf_op jit(solution)/shard_map/column_map/pallas_call | solution.py:130
  126.4 4.2 %column_map.2.refs_0_ = f32[40,64,128]{2,1,0:T(8,128)} custom-call(s32[32]{0:T(128)S(1)} %get-tuple-element.372.slot_ref, s32[32,128]{1,0:T(8,128)S(1)} %copy-done.6, f32[2,16,64,128]{3,2,1,0:T(8,128)S(1)} %get-tuple-element.346.refs_0_, f32[2,16,64,128]{3,2,1,0:T(8,128)} %collective-permute-done.42.refs_1_, f32[16,64,128]{2,1,0:T(8,128)} %collective-permute-done.43.refs_2_, ...), custom_call_target="tpu_custom_call" | custom-call | flops 1000000000 | bytes 4194304 | tf_op jit(solution)/shard_map/column_map/pallas_call | solution.py:130
  130.5 13.5 %conditional.29 = (f32[8,64,128]{2,1,0:T(8,128)}) conditional(s32[]{:T(128)} %clamp.15, () %tuple.213, (s32[]{:T(128)}, f32[40,64,128]{2,1,0:T(8,128)}) %tuple.214, (s32[]{:T(128)}, f32[40,64,128]{2,1,0:T(8,128)}) %tuple.214), branch_computations={%region_29.30_spmd, %region_30.31_spmd, %region_31.32_spmd} | conditional | flops 3 | bytes 1572950 | solution.py:243
  133.4 10.6 %collective-permute-done.17 = f32[8,64,128]{2,1,0:T(8,128)} collective-permute-done((f32[8,64,128]{2,1,0:T(8,128)S(1)}, f32[8,64,128]{2,1,0:T(8,128)}, u32[]{:S(2)}, u32[]{:S(2)}) %collective-permute-start.17) | collective-permute-done | bytes 262176 | tf_op jit(solution)/shard_map/cond/branch_2_fun/ppermute | solution.py:219
  144.1 14.1 %conditional.30 = (f32[8,64,128]{2,1,0:T(8,128)}) conditional(s32[]{:T(128)} %clamp.16, () %tuple.215, (s32[]{:T(128)}, f32[40,64,128]{2,1,0:T(8,128)}) %tuple.216, (s32[]{:T(128)}, f32[40,64,128]{2,1,0:T(8,128)}) %tuple.216), branch_computations={%region_32.33_spmd, %region_33.34_spmd, %region_34.35_spmd} | conditional | flops 3 | bytes 1572950 | solution.py:243
  147.0 11.2 %collective-permute-done.19 = f32[8,64,128]{2,1,0:T(8,128)} collective-permute-done((f32[8,64,128]{2,1,0:T(8,128)S(1)}, f32[8,64,128]{2,1,0:T(8,128)}, u32[]{:S(2)}, u32[]{:S(2)}) %collective-permute-start.19) | collective-permute-done | bytes 262176 | tf_op jit(solution)/shard_map/cond/branch_2_fun/ppermute | solution.py:219
  159.6 8.5 %conditional.33 = (f32[8,64,128]{2,1,0:T(8,128)}) conditional(s32[]{:T(128)} %clamp.19, () %tuple.221, (s32[]{:T(128)}, f32[40,64,128]{2,1,0:T(8,128)}) %tuple.222, (s32[]{:T(128)}, f32[40,64,128]{2,1,0:T(8,128)}) %tuple.222), branch_computations={%region_41.42_spmd, %region_42.43_spmd, %region_43.44_spmd} | conditional | flops 3 | bytes 1572950 | solution.py:243
  163.7 3.8 %collective-permute-done.24 = f32[4,64,128]{2,1,0:T(8,128)S(1)} collective-permute-done((f32[4,64,128]{2,1,0:T(8,128)S(1)}, f32[4,64,128]{2,1,0:T(8,128)S(1)}, u32[]{:S(2)}, u32[]{:S(2)}) %collective-permute-start.24) | collective-permute-done | bytes 131104 | tf_op jit(solution)/shard_map/cond/branch_1_fun/ppermute | solution.py:219
  168.1 6.4 %conditional.34 = (f32[8,64,128]{2,1,0:T(8,128)}) conditional(s32[]{:T(128)} %clamp.20, () %tuple.223, (s32[]{:T(128)}, f32[40,64,128]{2,1,0:T(8,128)}) %tuple.224, (s32[]{:T(128)}, f32[40,64,128]{2,1,0:T(8,128)}) %tuple.224), branch_computations={%region_44.45_spmd, %region_45.46_spmd, %region_46.47_spmd} | conditional | flops 3 | bytes 1572950 | solution.py:243
  174.5 10.6 %conditional.28 = (f32[8,64,128]{2,1,0:T(8,128)}) conditional(s32[]{:T(128)} %clamp.14, () %tuple.211, (s32[]{:T(128)}, f32[40,64,128]{2,1,0:T(8,128)}) %tuple.212, (s32[]{:T(128)}, f32[40,64,128]{2,1,0:T(8,128)}) %tuple.212), branch_computations={%region_26.27_spmd, %region_27.28_spmd, %region_28.29_spmd} | conditional | flops 3 | bytes 1572950 | solution.py:243
  177.3 7.8 %collective-permute-done.15 = f32[8,64,128]{2,1,0:T(8,128)} collective-permute-done((f32[8,64,128]{2,1,0:T(8,128)S(1)}, f32[8,64,128]{2,1,0:T(8,128)}, u32[]{:S(2)}, u32[]{:S(2)}) %collective-permute-start.15) | collective-permute-done | bytes 262176 | tf_op jit(solution)/shard_map/cond/branch_2_fun/ppermute | solution.py:219
  185.1 10.2 %conditional.22 = (f32[8,64,128]{2,1,0:T(8,128)}) conditional(s32[]{:T(128)} %clamp.15, () %tuple.199, (s32[]{:T(128)}, f32[40,64,128]{2,1,0:T(8,128)S(1)}) %tuple.325, (s32[]{:T(128)}, f32[40,64,128]{2,1,0:T(8,128)S(1)}) %tuple.326), branch_computations={%region_8.9_spmd, %region_9.10_spmd, %region_10.11_spmd} | conditional | flops 3 | bytes 1572950 | solution.py:243
  187.1 8.3 %collective-permute-done.3 = f32[8,64,128]{2,1,0:T(8,128)} collective-permute-done((f32[8,64,128]{2,1,0:T(8,128)S(1)}, f32[8,64,128]{2,1,0:T(8,128)}, u32[]{:S(2)}, u32[]{:S(2)}) %collective-permute-start.3) | collective-permute-done | bytes 262176 | tf_op jit(solution)/shard_map/cond/branch_2_fun/ppermute | solution.py:219
  195.3 11.6 %conditional.23 = (f32[8,64,128]{2,1,0:T(8,128)}) conditional(s32[]{:T(128)} %clamp.16, () %tuple.201, (s32[]{:T(128)}, f32[40,64,128]{2,1,0:T(8,128)S(1)}) %tuple.327, (s32[]{:T(128)}, f32[40,64,128]{2,1,0:T(8,128)S(1)}) %tuple.328), branch_computations={%region_11.12_spmd, %region_12.13_spmd, %region_13.14_spmd} | conditional | flops 3 | bytes 1572950 | solution.py:243
  197.3 9.7 %collective-permute-done.5 = f32[8,64,128]{2,1,0:T(8,128)} collective-permute-done((f32[8,64,128]{2,1,0:T(8,128)S(1)}, f32[8,64,128]{2,1,0:T(8,128)}, u32[]{:S(2)}, u32[]{:S(2)}) %collective-permute-start.5) | collective-permute-done | bytes 262176 | tf_op jit(solution)/shard_map/cond/branch_2_fun/ppermute | solution.py:219
  208.4 7.6 %conditional.26 = (f32[8,64,128]{2,1,0:T(8,128)}) conditional(s32[]{:T(128)} %clamp.19, () %tuple.207, (s32[]{:T(128)}, f32[40,64,128]{2,1,0:T(8,128)S(1)}) %tuple.333, (s32[]{:T(128)}, f32[40,64,128]{2,1,0:T(8,128)S(1)}) %tuple.334), branch_computations={%region_20.21_spmd, %region_21.22_spmd, %region_22.23_spmd} | conditional | flops 3 | bytes 1572950 | solution.py:243
  216.0 5.5 %conditional.27 = (f32[8,64,128]{2,1,0:T(8,128)}) conditional(s32[]{:T(128)} %clamp.20, () %tuple.209, (s32[]{:T(128)}, f32[40,64,128]{2,1,0:T(8,128)S(1)}) %tuple.335, (s32[]{:T(128)}, f32[40,64,128]{2,1,0:T(8,128)S(1)}) %tuple.336), branch_computations={%region_23.24_spmd, %region_24.25_spmd, %region_25.26_spmd} | conditional | flops 3 | bytes 1572950 | solution.py:243
  221.5 9.6 %conditional.21 = (f32[8,64,128]{2,1,0:T(8,128)}) conditional(s32[]{:T(128)} %clamp.14, () %tuple.197, (s32[]{:T(128)}, f32[40,64,128]{2,1,0:T(8,128)S(1)}) %tuple.337, (s32[]{:T(128)}, f32[40,64,128]{2,1,0:T(8,128)S(1)}) %tuple.338), branch_computations={%region_5.6_spmd, %region_6.7_spmd, %region_7.8_spmd} | conditional | flops 3 | bytes 1572950 | solution.py:243
  223.6 7.6 %collective-permute-done.1 = f32[8,64,128]{2,1,0:T(8,128)} collective-permute-done((f32[8,64,128]{2,1,0:T(8,128)S(1)}, f32[8,64,128]{2,1,0:T(8,128)}, u32[]{:S(2)}, u32[]{:S(2)}) %collective-permute-start.1) | collective-permute-done | bytes 262176 | tf_op jit(solution)/shard_map/cond/branch_2_fun/ppermute | solution.py:219
  (107 shorter events, 73.4 us)
Async XLA Ops:
  8.9 8.2 %copy-start.1 = (f32[2,16,64,128]{3,2,1,0:T(8,128)}, f32[2,16,64,128]{3,2,1,0:T(8,128)S(1)}, u32[]{:S(2)}) copy-start(f32[2,16,64,128]{3,2,1,0:T(8,128)S(1)} %get-tuple-element.350.refs_0_) | copy-start | bytes 3145732
  8.9 27.2 %collective-permute-start.46 = (f32[2,16,64,128]{3,2,1,0:T(8,128)}, f32[2,16,64,128]{3,2,1,0:T(8,128)}, u32[]{:S(2)}, u32[]{:S(2)}) collective-permute-start(f32[2,16,64,128]{3,2,1,0:T(8,128)} %get-tuple-element.351), channel_id=1, source_target_pairs={{0,8},{8,0},{16,24},{24,16},{1,9},{9,1},{17,25},{25,17},{2,10},{10... | collective-permute-start | bytes 3145736 | tf_op jit(solution)/shard_map/ppermute | solution.py:288
  11.8 5.8 %copy-start.12 = (s32[32]{0:T(128)S(1)}, s32[32]{0:T(128)}, u32[]{:S(2)}) copy-start(s32[32]{0:T(128)} %param.76) | copy-start | bytes 388
  11.8 28.4 %collective-permute-start.48 = (f32[2,16,64,128]{3,2,1,0:T(8,128)}, f32[2,16,64,128]{3,2,1,0:T(8,128)}, u32[]{:S(2)}, u32[]{:S(2)}) collective-permute-start(f32[2,16,64,128]{3,2,1,0:T(8,128)} %get-tuple-element.353), channel_id=1, source_target_pairs={{0,16},{8,24},{16,0},{24,8},{1,17},{9,25},{17,1},{25,9},{2,18},{10... | collective-permute-start | bytes 3145736 | tf_op jit(solution)/shard_map/ppermute | solution.py:289
  17.0 43.5 %collective-permute-start.44 = (f32[2,16,64,128]{3,2,1,0:T(8,128)}, f32[2,16,64,128]{3,2,1,0:T(8,128)S(1)}, u32[]{:S(2)}, u32[]{:S(2)}) collective-permute-start(f32[2,16,64,128]{3,2,1,0:T(8,128)} %get-tuple-element.349), channel_id=1, source_target_pairs={{0,16},{8,24},{16,0},{24,8},{1,17},{9,25},{17,1},{25,9},{2,18},{10... | collective-permute-start | bytes 3145736 | tf_op jit(solution)/shard_map/ppermute | solution.py:289
  17.5 43.9 %collective-permute-start.42 = (f32[2,16,64,128]{3,2,1,0:T(8,128)}, f32[2,16,64,128]{3,2,1,0:T(8,128)}, u32[]{:S(2)}, u32[]{:S(2)}) collective-permute-start(f32[2,16,64,128]{3,2,1,0:T(8,128)} %get-tuple-element.347), channel_id=1, source_target_pairs={{0,8},{8,0},{16,24},{24,16},{1,9},{9,1},{17,25},{25,17},{2,10},{10... | collective-permute-start | bytes 3145736 | tf_op jit(solution)/shard_map/ppermute | solution.py:288
  23.1 17.2 %copy-start.4 = (f32[2,16,64,128]{3,2,1,0:T(8,128)S(1)}, f32[2,16,64,128]{3,2,1,0:T(8,128)}, u32[]{:S(2)}) copy-start(f32[2,16,64,128]{3,2,1,0:T(8,128)} %copy-done.3) | copy-start | bytes 3145732
  38.2 83.9 %collective-permute-start.47 = (f32[16,64,128]{2,1,0:T(8,128)}, f32[16,64,128]{2,1,0:T(8,128)}, u32[]{:S(2)}, u32[]{:S(2)}) collective-permute-start(f32[16,64,128]{2,1,0:T(8,128)} %fusion.1), channel_id=1, source_target_pairs={{0,16},{8,24},{16,0},{24,8},{1,17},{9,25},{17,1},{25,9},{2,18},{10... | collective-permute-start | bytes 1572872 | tf_op jit(solution)/shard_map/ppermute | solution.py:290
  42.2 79.9 %collective-permute-start.49 = (f32[16,64,128]{2,1,0:T(8,128)}, f32[16,64,128]{2,1,0:T(8,128)}, u32[]{:S(2)}, u32[]{:S(2)}) collective-permute-start(f32[16,64,128]{2,1,0:T(8,128)} %fusion), channel_id=1, source_target_pairs={{0,8},{8,0},{16,24},{24,16},{1,9},{9,1},{17,25},{25,17},{2,10},{10... | collective-permute-start | bytes 1572872 | tf_op jit(solution)/shard_map/ppermute | solution.py:291
  60.6 4.9 %copy-start.6 = (s32[32,128]{1,0:T(8,128)S(1)}, s32[32,128]{1,0:T(8,128)}, u32[]{:S(2)}) copy-start(s32[32,128]{1,0:T(8,128)} %col_ref.5) | copy-start | bytes 49156
  60.6 4.9 %copy-start.9 = (f32[4096,64]{0,1:T(8,128)S(1)}, f32[4096,64]{0,1:T(8,128)}, u32[]{:S(2)}) copy-start(f32[4096,64]{0,1:T(8,128)} %param.71) | copy-start | bytes 3145732
  61.5 64.9 %collective-permute-start.45 = (f32[16,64,128]{2,1,0:T(8,128)}, f32[16,64,128]{2,1,0:T(8,128)}, u32[]{:S(2)}, u32[]{:S(2)}) collective-permute-start(f32[16,64,128]{2,1,0:T(8,128)} %fusion.2), channel_id=1, source_target_pairs={{0,8},{8,0},{16,24},{24,16},{1,9},{9,1},{17,25},{25,17},{2,10},{10... | collective-permute-start | bytes 1572872 | tf_op jit(solution)/shard_map/ppermute | solution.py:291
  63.4 63.0 %collective-permute-start.43 = (f32[16,64,128]{2,1,0:T(8,128)}, f32[16,64,128]{2,1,0:T(8,128)}, u32[]{:S(2)}, u32[]{:S(2)}) collective-permute-start(f32[16,64,128]{2,1,0:T(8,128)} %fusion.3), channel_id=1, source_target_pairs={{0,16},{8,24},{16,0},{24,8},{1,17},{9,25},{17,1},{25,9},{2,18},{10... | collective-permute-start | bytes 1572872 | tf_op jit(solution)/shard_map/ppermute | solution.py:290
  70.6 7.8 %collective-permute-start.29 = (f32[8,64,128]{2,1,0:T(8,128)S(1)}, f32[8,64,128]{2,1,0:T(8,128)}, u32[]{:S(2)}, u32[]{:S(2)}) collective-permute-start(f32[8,64,128]{2,1,0:T(8,128)S(1)} %constant_dynamic-slice_fusion.29), channel_id=1, source_target_pairs={{0,1},{1,2},{2,3},{3,4},{4,5},{5,6},{6,7},{7,0},{8,9},{9,10},{10,1... | collective-permute-start | bytes 786440 | tf_op jit(solution)/shard_map/cond/branch_2_fun/ppermute | solution.py:219
  81.2 8.3 %collective-permute-start.31 = (f32[8,64,128]{2,1,0:T(8,128)S(1)}, f32[8,64,128]{2,1,0:T(8,128)}, u32[]{:S(2)}, u32[]{:S(2)}) collective-permute-start(f32[8,64,128]{2,1,0:T(8,128)S(1)} %constant_dynamic-slice_fusion.31), channel_id=1, source_target_pairs={{0,2},{1,3},{2,4},{3,5},{4,6},{5,7},{6,0},{7,1},{8,10},{9,11},{10,... | collective-permute-start | bytes 786440 | tf_op jit(solution)/shard_map/cond/branch_2_fun/ppermute | solution.py:219
  92.4 10.1 %collective-permute-start.33 = (f32[8,64,128]{2,1,0:T(8,128)S(1)}, f32[8,64,128]{2,1,0:T(8,128)}, u32[]{:S(2)}, u32[]{:S(2)}) collective-permute-start(f32[8,64,128]{2,1,0:T(8,128)S(1)} %constant_dynamic-slice_fusion.33), channel_id=1, source_target_pairs={{0,3},{1,4},{2,5},{3,6},{4,7},{5,0},{6,1},{7,2},{8,11},{9,12},{10,... | collective-permute-start | bytes 786440 | tf_op jit(solution)/shard_map/cond/branch_2_fun/ppermute | solution.py:219
  104.0 14.8 %copy-start.13 = (s32[32]{0:T(128)S(1)}, s32[32]{0:T(128)}, u32[]{:S(2)}) copy-start(s32[32]{0:T(128)} %param.75) | copy-start | bytes 388
  106.8 5.0 %collective-permute-start.38 = (f32[4,64,128]{2,1,0:T(8,128)S(1)}, f32[4,64,128]{2,1,0:T(8,128)S(1)}, u32[]{:S(2)}, u32[]{:S(2)}) collective-permute-start(f32[4,64,128]{2,1,0:T(8,128)S(1)} %constant_dynamic-slice_fusion.38), channel_id=1, source_target_pairs={{0,6},{1,7},{2,0},{3,1},{4,2},{5,3},{6,4},{7,5},{8,14},{9,15},{10,... | collective-permute-start | bytes 393224 | tf_op jit(solution)/shard_map/cond/branch_1_fun/ppermute | solution.py:219
  115.5 2.6 %collective-permute-start.40 = (f32[4,64,128]{2,1,0:T(8,128)S(1)}, f32[4,64,128]{2,1,0:T(8,128)S(1)}, u32[]{:S(2)}, u32[]{:S(2)}) collective-permute-start(f32[4,64,128]{2,1,0:T(8,128)S(1)} %constant_dynamic-slice_fusion.40), channel_id=1, source_target_pairs={{0,7},{1,0},{2,1},{3,2},{4,3},{5,4},{6,5},{7,6},{8,15},{9,8},{10,9... | collective-permute-start | bytes 393224 | tf_op jit(solution)/shard_map/cond/branch_1_fun/ppermute | solution.py:219
  119.0 3.1 %copy-start.5 = (f32[2,16,64,128]{3,2,1,0:T(8,128)S(1)}, f32[2,16,64,128]{3,2,1,0:T(8,128)}, u32[]{:S(2)}) copy-start(f32[2,16,64,128]{3,2,1,0:T(8,128)} %copy-done.3) | copy-start | bytes 3145732
  133.4 10.7 %collective-permute-start.17 = (f32[8,64,128]{2,1,0:T(8,128)S(1)}, f32[8,64,128]{2,1,0:T(8,128)}, u32[]{:S(2)}, u32[]{:S(2)}) collective-permute-start(f32[8,64,128]{2,1,0:T(8,128)S(1)} %constant_dynamic-slice_fusion.17), channel_id=1, source_target_pairs={{0,2},{1,3},{2,4},{3,5},{4,6},{5,7},{6,0},{7,1},{8,10},{9,11},{10,... | collective-permute-start | bytes 786440 | tf_op jit(solution)/shard_map/cond/branch_2_fun/ppermute | solution.py:219
  146.9 11.3 %collective-permute-start.19 = (f32[8,64,128]{2,1,0:T(8,128)S(1)}, f32[8,64,128]{2,1,0:T(8,128)}, u32[]{:S(2)}, u32[]{:S(2)}) collective-permute-start(f32[8,64,128]{2,1,0:T(8,128)S(1)} %constant_dynamic-slice_fusion.19), channel_id=1, source_target_pairs={{0,3},{1,4},{2,5},{3,6},{4,7},{5,0},{6,1},{7,2},{8,11},{9,12},{10,... | collective-permute-start | bytes 786440 | tf_op jit(solution)/shard_map/cond/branch_2_fun/ppermute | solution.py:219
  162.4 5.0 %collective-permute-start.24 = (f32[4,64,128]{2,1,0:T(8,128)S(1)}, f32[4,64,128]{2,1,0:T(8,128)S(1)}, u32[]{:S(2)}, u32[]{:S(2)}) collective-permute-start(f32[4,64,128]{2,1,0:T(8,128)S(1)} %constant_dynamic-slice_fusion.24), channel_id=1, source_target_pairs={{0,6},{1,7},{2,0},{3,1},{4,2},{5,3},{6,4},{7,5},{8,14},{9,15},{10,... | collective-permute-start | bytes 393224 | tf_op jit(solution)/shard_map/cond/branch_1_fun/ppermute | solution.py:219
  168.1 17.0 %copy-start.11 = (f32[40,64,128]{2,1,0:T(8,128)S(1)}, f32[40,64,128]{2,1,0:T(8,128)}, u32[]{:S(2)}) copy-start(f32[40,64,128]{2,1,0:T(8,128)} %column_map.2.refs_0_) | copy-start | bytes 3932164
  171.2 2.6 %collective-permute-start.26 = (f32[4,64,128]{2,1,0:T(8,128)S(1)}, f32[4,64,128]{2,1,0:T(8,128)S(1)}, u32[]{:S(2)}, u32[]{:S(2)}) collective-permute-start(f32[4,64,128]{2,1,0:T(8,128)S(1)} %constant_dynamic-slice_fusion.26), channel_id=1, source_target_pairs={{0,7},{1,0},{2,1},{3,2},{4,3},{5,4},{6,5},{7,6},{8,15},{9,8},{10,9... | collective-permute-start | bytes 393224 | tf_op jit(solution)/shard_map/cond/branch_1_fun/ppermute | solution.py:219
  177.2 7.9 %collective-permute-start.15 = (f32[8,64,128]{2,1,0:T(8,128)S(1)}, f32[8,64,128]{2,1,0:T(8,128)}, u32[]{:S(2)}, u32[]{:S(2)}) collective-permute-start(f32[8,64,128]{2,1,0:T(8,128)S(1)} %constant_dynamic-slice_fusion.15), channel_id=1, source_target_pairs={{0,1},{1,2},{2,3},{3,4},{4,5},{5,6},{6,7},{7,0},{8,9},{9,10},{10,1... | collective-permute-start | bytes 786440 | tf_op jit(solution)/shard_map/cond/branch_2_fun/ppermute | solution.py:219
  187.0 8.3 %collective-permute-start.3 = (f32[8,64,128]{2,1,0:T(8,128)S(1)}, f32[8,64,128]{2,1,0:T(8,128)}, u32[]{:S(2)}, u32[]{:S(2)}) collective-permute-start(f32[8,64,128]{2,1,0:T(8,128)S(1)} %constant_dynamic-slice_fusion.3), channel_id=1, source_target_pairs={{0,2},{1,3},{2,4},{3,5},{4,6},{5,7},{6,0},{7,1},{8,10},{9,11},{10,... | collective-permute-start | bytes 786440 | tf_op jit(solution)/shard_map/cond/branch_2_fun/ppermute | solution.py:219
  197.2 9.7 %collective-permute-start.5 = (f32[8,64,128]{2,1,0:T(8,128)S(1)}, f32[8,64,128]{2,1,0:T(8,128)}, u32[]{:S(2)}, u32[]{:S(2)}) collective-permute-start(f32[8,64,128]{2,1,0:T(8,128)S(1)} %constant_dynamic-slice_fusion.5), channel_id=1, source_target_pairs={{0,3},{1,4},{2,5},{3,6},{4,7},{5,0},{6,1},{7,2},{8,11},{9,12},{10,... | collective-permute-start | bytes 786440 | tf_op jit(solution)/shard_map/cond/branch_2_fun/ppermute | solution.py:219
  210.2 5.0 %collective-permute-start.10 = (f32[4,64,128]{2,1,0:T(8,128)S(1)}, f32[4,64,128]{2,1,0:T(8,128)S(1)}, u32[]{:S(2)}, u32[]{:S(2)}) collective-permute-start(f32[4,64,128]{2,1,0:T(8,128)S(1)} %constant_dynamic-slice_fusion.10), channel_id=1, source_target_pairs={{0,6},{1,7},{2,0},{3,1},{4,2},{5,3},{6,4},{7,5},{8,14},{9,15},{10,... | collective-permute-start | bytes 393224 | tf_op jit(solution)/shard_map/cond/branch_1_fun/ppermute | solution.py:219
  216.0 15.2 %copy-start.10 = (f32[40,64,128]{2,1,0:T(8,128)S(1)}, f32[40,64,128]{2,1,0:T(8,128)}, u32[]{:S(2)}) copy-start(f32[40,64,128]{2,1,0:T(8,128)} %column_map.3.refs_0_) | copy-start | bytes 3932164
  218.2 2.6 %collective-permute-start.12 = (f32[4,64,128]{2,1,0:T(8,128)S(1)}, f32[4,64,128]{2,1,0:T(8,128)S(1)}, u32[]{:S(2)}, u32[]{:S(2)}) collective-permute-start(f32[4,64,128]{2,1,0:T(8,128)S(1)} %constant_dynamic-slice_fusion.12), channel_id=1, source_target_pairs={{0,7},{1,0},{2,1},{3,2},{4,3},{5,4},{6,5},{7,6},{8,15},{9,8},{10,9... | collective-permute-start | bytes 393224 | tf_op jit(solution)/shard_map/cond/branch_1_fun/ppermute | solution.py:219
  223.3 7.9 %collective-permute-start.1 = (f32[8,64,128]{2,1,0:T(8,128)S(1)}, f32[8,64,128]{2,1,0:T(8,128)}, u32[]{:S(2)}, u32[]{:S(2)}) collective-permute-start(f32[8,64,128]{2,1,0:T(8,128)S(1)} %constant_dynamic-slice_fusion.1), channel_id=1, source_target_pairs={{0,1},{1,2},{2,3},{3,4},{4,5},{5,6},{6,7},{7,0},{8,9},{9,10},{10,1... | collective-permute-start | bytes 786440 | tf_op jit(solution)/shard_map/cond/branch_2_fun/ppermute | solution.py:219
  (5 other events, 7.6 us)

commit v2 on v1

v2 whole, which is shorter than its diff:
```python
import functools
import jax
import jax.numpy as jnp
from jax import lax
from jax.experimental import pallas as pl
from jax.experimental.pallas import tpu as pltpu
from jax.sharding import PartitionSpec as P

TILE = 128
GROUPS = 4
ANY = pl.BlockSpec(memory_space=pl.ANY)
VMEM = pl.BlockSpec(memory_space=pltpu.VMEM)
SMEM = pl.BlockSpec(memory_space=pltpu.SMEM)


def split16(x):
    high = x.astype(jnp.bfloat16)
    low = (x - high.astype(jnp.float32)).astype(jnp.bfloat16)
    return high, low


def rows_kernel(first, rows, step_blocks, pair_ref, slot_ref, *refs):
    tiles = refs[: 2 * step_blocks]
    send_x, keep_x, send_y, keep_y, onehot = refs[2 * step_blocks :]

    @pl.when(pl.program_id(0) == 0)
    def _():
        group = lax.axis_index("grp")
        keys = []
        for r in range(2):
            owner = jnp.int32(0)
            for h in range(2 * GROUPS):
                owner = jnp.where(pair_ref[h] == 2 * group + r, h // 2, owner)
            away = jnp.bitwise_xor(owner, group)
            local = slot_ref[r : r + 1, :] - first
            inside = jnp.logical_and(local >= 0, local < rows)
            keys.append(jnp.where(inside, away * rows + local, -1))
        key = jnp.concatenate(keys + keys, axis=1)
        place = lax.broadcasted_iota(jnp.int32, (GROUPS * rows, 4 * TILE), 0)
        onehot[...] = (place == key).astype(jnp.float32).astype(jnp.bfloat16)

    def mapped(pair):
        x = jnp.concatenate([tile[0] for tile in pair], axis=1)
        high, low = split16(x)
        both = jnp.concatenate([high, low], axis=0)
        return jnp.dot(onehot[...], both, preferred_element_type=jnp.float32)

    for i in range(0, step_blocks, 2):
        full = mapped(tiles[i : i + 2])
        for j in range(2):
            lanes = slice(j * TILE, (j + 1) * TILE)
            part = [full[m * rows : (m + 1) * rows, lanes] for m in range(GROUPS)]
            keep_x[0, i + j], send_x[0, i + j], keep_x[1, i + j], send_x[1, i + j] = part
        full = mapped(tiles[step_blocks + i : step_blocks + i + 2])
        for j in range(2):
            lanes = slice(j * TILE, (j + 1) * TILE)
            part = [full[m * rows : (m + 1) * rows, lanes] for m in range(GROUPS)]
            keep_y[0, i + j], keep_y[1, i + j], send_y[0, i + j], send_y[1, i + j] = part


def row_map(adjacency, row_slot, row_pair, first, rows):
    blocks, own_rows, tile = adjacency.shape
    half = blocks // 2
    step_blocks = 4
    steps = half // step_blocks

    def at(base, j):
        return pl.BlockSpec((1, own_rows, tile), lambda i: (base + step_blocks * i + j, 0, 0))

    out = jax.ShapeDtypeStruct((2, half, rows, tile), jnp.float32)
    return pl.pallas_call(
        functools.partial(rows_kernel, first, rows, step_blocks),
        grid=(steps,),
        out_shape=[out] * 4,
        in_specs=[SMEM, VMEM]
        + [at(0, j) for j in range(step_blocks)]
        + [at(half, j) for j in range(step_blocks)],
        out_specs=[pl.BlockSpec((2, step_blocks, rows, tile), lambda i: (0, i, 0, 0))] * 4,
        scratch_shapes=[pltpu.VMEM((GROUPS * rows, 4 * tile), jnp.bfloat16)],
        compiler_params=pltpu.CompilerParams(vmem_limit_bytes=32 << 20),
        cost_estimate=pl.CostEstimate(flops=int(2e9), bytes_accessed=12 << 20, transcendentals=0),
        name="row_map",
    )(row_pair, row_slot, *([adjacency] * (2 * step_blocks)))


def lanes_of(x, slots):
    place = lax.broadcasted_iota(jnp.int32, (TILE, TILE), 0)
    onehot = (place == slots).astype(jnp.float32).astype(jnp.bfloat16)
    high, low = split16(x)
    both = lax.dot_general(
        jnp.concatenate([high, low], axis=0),
        onehot,
        (((1,), (1,)), ((), ())),
        preferred_element_type=jnp.float32,
    )
    return both[: x.shape[0]] + both[x.shape[0] :]


def write_units(held, outs, sem, full):
    copies = []
    for n, out in enumerate(outs):
        size = out.shape[0]
        at = n * size if n < full else (n - full + 1) * 2 * size
        copies.append(pltpu.make_async_copy(held.at[pl.ds(at, size)], out, sem.at[n]))
    for copy in copies:
        copy.start()
    for copy in copies:
        copy.wait()


def features_kernel(blocks, full, slot_ref, col_ref, x_ref, *refs):
    outs, held, sem = refs[:-2], refs[-2], refs[-1]
    for p in range(blocks):
        lanes = slice(p * TILE, (p + 1) * TILE)
        held[slot_ref[p]] = lanes_of(x_ref[:, lanes], col_ref[p : p + 1, :])
    write_units(held, outs, sem, full)


def columns_kernel(step_blocks, steps, full, slot_ref, col_ref, *refs):
    ins, outs, held, sem = refs[:6], refs[6:-2], refs[-2], refs[-1]
    i = pl.program_id(0)
    for half in range(2):
        keep, got1, got2 = ins[3 * half : 3 * half + 3]
        for j in range(step_blocks):
            p = half * steps * step_blocks + i * step_blocks + j
            x = keep[0, j] + got1[0, j] + got2[j]
            held[slot_ref[p]] = lanes_of(x, col_ref[pl.ds(p, 1), :])

    @pl.when(i == steps - 1)
    def _():
        write_units(held, outs, sem, full)


def unit_outputs(full, size, rows):
    half = full - 1
    shapes = [(size, rows, TILE)] * full + [(size // 2, rows, TILE)] * half
    return dict(
        out_shape=[jax.ShapeDtypeStruct(shape, jnp.float32) for shape in shapes],
        out_specs=[ANY] * (full + half),
        scratch_shapes=[
            pltpu.VMEM((full * size, rows, TILE), jnp.float32),
            pltpu.SemaphoreType.DMA((full + half,)),
        ],
    )


def column_map(keep_x, got1_x, got2_x, keep_y, got1_y, got2_y, col_slot, slot, full, size):
    half, rows, tile = got2_x.shape
    step_blocks = 4
    steps = half // step_blocks
    four = pl.BlockSpec((1, step_blocks, rows, tile), lambda i: (0, i, 0, 0))
    three = pl.BlockSpec((step_blocks, rows, tile), lambda i: (i, 0, 0))
    return pl.pallas_call(
        functools.partial(columns_kernel, step_blocks, steps, full),
        grid=(steps,),
        in_specs=[SMEM, VMEM] + [four, four, three] * 2,
        compiler_params=pltpu.CompilerParams(vmem_limit_bytes=32 << 20),
        cost_estimate=pl.CostEstimate(flops=int(1e9), bytes_accessed=4 << 20, transcendentals=0),
        name="column_map",
        **unit_outputs(full, size, rows),
    )(slot, col_slot, keep_x, got1_x, got2_x, keep_y, got1_y, got2_y)


def feature_map(features_t, col_slot, slot, full, size):
    width, columns = features_t.shape
    blocks = columns // TILE
    return pl.pallas_call(
        functools.partial(features_kernel, blocks, full),
        in_specs=[SMEM, VMEM, VMEM],
        compiler_params=pltpu.CompilerParams(vmem_limit_bytes=32 << 20),
        cost_estimate=pl.CostEstimate(flops=int(1e9), bytes_accessed=2 << 20, transcendentals=0),
        name="feature_map",
        **unit_outputs(full, size, width),
    )(slot, col_slot, features_t)


def merge_kernel(count_in, in_lanes, src_ref, *refs):
    pieces = refs[:count_in]
    out_ref, held, sem = refs[-3:]
    copies = []
    at = 0
    for n, piece in enumerate(pieces):
        size = piece.shape[0]
        copies.append(pltpu.make_async_copy(piece, held.at[pl.ds(at, size)], sem.at[n]))
        at += size
    for copy in copies:
        copy.start()
    for copy in copies:
        copy.wait()
    for k in range(src_ref.shape[0] // 2):
        total = held[src_ref[2 * k]] + held[src_ref[2 * k + 1]]
        if in_lanes:
            out_ref[:, k * TILE : (k + 1) * TILE] = total
        else:
            out_ref[k] = total


def merge_scratch(pieces):
    _, rows, tile = pieces[0].shape
    return [
        pltpu.VMEM((sum(piece.shape[0] for piece in pieces), rows, tile), jnp.float32),
        pltpu.SemaphoreType.DMA((len(pieces),)),
    ]


def merge_features(pieces, src):
    width = pieces[0].shape[1]
    count = src.shape[0] // 2
    return pl.pallas_call(
        functools.partial(merge_kernel, len(pieces), True),
        out_shape=jax.ShapeDtypeStruct((width, count * TILE), jnp.float32),
        in_specs=[SMEM] + [ANY] * len(pieces),
        out_specs=VMEM,
        scratch_shapes=merge_scratch(pieces),
        compiler_params=pltpu.CompilerParams(vmem_limit_bytes=32 << 20),
        cost_estimate=pl.CostEstimate(flops=int(1e6), bytes_accessed=3 << 20, transcendentals=0),
        name="merge_features",
    )(src, *pieces)


def merge_tiles(pieces, src, first, before):
    rows = pieces[0].shape[1]
    count = src.shape[0] // 2
    operands = (src, *pieces) + (() if before is None else (before,))
    return pl.pallas_call(
        functools.partial(merge_kernel, len(pieces), False),
        grid=(1,),
        out_shape=jax.ShapeDtypeStruct((count, TILE, TILE), jnp.float32),
        in_specs=[SMEM] + [ANY] * (len(operands) - 1),
        out_specs=pl.BlockSpec((count, rows, TILE), lambda i: (0, first // rows, 0)),
        input_output_aliases={} if before is None else {len(operands) - 1: 0},
        scratch_shapes=merge_scratch(pieces),
        compiler_params=pltpu.CompilerParams(vmem_limit_bytes=32 << 20),
        cost_estimate=pl.CostEstimate(flops=int(1e6), bytes_accessed=3 << 20, transcendentals=0),
        name="merge_tiles",
    )(*operands)


SETS = ((1, 4, 7), (2, 6), (3, 5))


def turn(x, shift, dev_count):
    return lax.ppermute(x, "dev", [(i, (i + shift) % dev_count) for i in range(dev_count)])


def unwritten(shapes):
    return pl.pallas_call(
        lambda *refs: None,
        out_shape=[jax.ShapeDtypeStruct(shape, jnp.float32) for shape in shapes],
        out_specs=[ANY] * len(shapes),
        cost_estimate=pl.CostEstimate(flops=0, bytes_accessed=0, transcendentals=0),
        name="unwritten",
    )()


def exchange_set(which, units, choice, dev_count):
    shifts = SETS[which]
    operands = [units[n] for shift in shifts for n in (shift, dev_count - 1 + shift)]

    def branch(code):
        used = [code // 3**i % 3 for i in range(len(shifts))]
        sent = [(u == 2, u == 1) for u in used]
        sent = [flag for pair in sent for flag in pair]

        def run(*arrays):
            rest = list(unwritten([x.shape for x, flag in zip(arrays, sent) if not flag]))
            got = []
            for n, (array, flag) in enumerate(zip(arrays, sent)):
                got.append(turn(array, shifts[n // 2], dev_count) if flag else rest.pop(0))
            return got

        return run

    return lax.switch(choice[which], [branch(c) for c in range(3 ** len(shifts))], *operands)


def exchange_all(blocks, capacity, dev_count):
    me = lax.axis_index("dev")
    ids = jnp.arange(dev_count * capacity, dtype=jnp.int32)
    away, place = ids // capacity, ids % capacity
    send = jnp.take(blocks, (away - me) % dev_count * capacity + place, axis=0)
    got = lax.all_to_all(send, "dev", split_axis=0, concat_axis=0, tiled=True)
    return jnp.take(got, (me - away) % dev_count * capacity + place, axis=0)


def ordered(first, then):
    first, then = lax.optimization_barrier((first, then))
    return first, then


def body(adjacency, features, col_slot, row_slot, row_pair, col_pair, col_offset):
    dev_count = lax.axis_size("dev")
    blocks = adjacency.shape[0]
    capacity = 2 * blocks // dev_count
    in_sets = dev_count == 8
    full, size = (dev_count, capacity) if in_sets else (1, capacity * dev_count)

    positions = jnp.arange(blocks, dtype=jnp.int32)
    same = col_offset[:, None] == col_offset[None, :]
    earlier = positions[None, :] < positions[:, None]
    rank = jnp.sum(jnp.logical_and(same, earlier).astype(jnp.int32), axis=1)
    slot = col_offset * capacity + rank
    offsets = jnp.arange(dev_count, dtype=jnp.int32)
    counts = jnp.sum((col_offset[None, :] == offsets[:, None]).astype(jnp.int32), axis=1)
    used = (counts > 0).astype(jnp.int32) + (counts > capacity // 2).astype(jnp.int32)
    where = slot
    if in_sets:
        few = jnp.sum(same.astype(jnp.int32), axis=1) <= capacity // 2
        in_half = capacity * dev_count + (col_offset - 1) * (capacity // 2) + rank
        where = jnp.where(jnp.logical_and(few, col_offset > 0), in_half, slot)
    chosen = col_pair[:, None] == positions[None, :]
    src = jnp.sum(jnp.where(chosen, where[None, :], 0), axis=1)

    x_side = [(g, g ^ 1) for g in range(GROUPS)]
    y_side = [(g, g ^ 2) for g in range(GROUPS)]

    def first_step(maps):
        return lax.ppermute(maps[0], "grp", x_side), lax.ppermute(maps[2], "grp", y_side)

    def partial_sums(maps, got):
        return maps[1][1] + got[0][1], maps[3][1] + got[1][1]

    def second_step(sums):
        return lax.ppermute(sums[0], "grp", y_side), lax.ppermute(sums[1], "grp", x_side)

    def columns(maps, got1, got2):
        return column_map(
            maps[1], got1[0], got2[0], maps[3], got1[1], got2[1], col_slot, slot, full, size
        )

    rows = TILE // 2
    maps_a = row_map(adjacency, row_slot, row_pair, 0, rows)
    got1_a = first_step(maps_a)
    maps_a, units_x = ordered(maps_a, feature_map(features.T, col_slot, slot, full, size))

    if not in_sets:
        maps_b = row_map(adjacency, row_slot, row_pair, rows, rows)
        coarse_adjacency = None
        got_x = exchange_all(units_x[0], capacity, dev_count)
        for first, maps in ((0, maps_a), (rows, maps_b)):
            got1 = got1_a if first == 0 else first_step(maps)
            units = columns(maps, got1, second_step(partial_sums(maps, got1)))
            got = exchange_all(units[0], capacity, dev_count)
            coarse_adjacency = merge_tiles([got], src, first, coarse_adjacency)
        return coarse_adjacency, merge_features([got_x], src).T

    weights = [[0] * dev_count for _ in SETS]
    for w, shifts in zip(weights, SETS):
        for i, shift in enumerate(shifts):
            w[shift] = 3**i
    choice = jnp.sum(jnp.array(weights, dtype=jnp.int32) * used[None, :], axis=1)

    def collect(units, parts):
        pieces = list(units)
        for shifts, part in zip(SETS, parts):
            for i, shift in enumerate(shifts):
                pieces[shift], pieces[dev_count - 1 + shift] = part[2 * i], part[2 * i + 1]
        return pieces

    maps_b = row_map(adjacency, row_slot, row_pair, rows, rows)
    maps_b, units_x = ordered(maps_b, units_x)
    part_x = [exchange_set(which, units_x, choice, dev_count) for which in (0, 1)]
    (part_x, maps_b), got1_a = ordered((part_x, maps_b), got1_a)
    sums_a = partial_sums(maps_a, got1_a)
    sums_a, units_x = ordered(sums_a, units_x)
    got2_a = second_step(sums_a)
    part_x.append(exchange_set(2, units_x, choice, dev_count))
    (part_x, maps_b), got2_a = ordered((part_x, maps_b), got2_a)
    got1_b = first_step(maps_b)
    units_a = columns(maps_a, got1_a, got2_a)
    part_a = [exchange_set(which, units_a, choice, dev_count) for which in (0, 1)]
    part_a, got1_b = ordered(part_a, got1_b)
    sums_b = partial_sums(maps_b, got1_b)
    sums_b, units_a = ordered(sums_b, units_a)
    got2_b = second_step(sums_b)
    part_a.append(exchange_set(2, units_a, choice, dev_count))
    part_a, got2_b = ordered(part_a, got2_b)
    units_b = columns(maps_b, got1_b, got2_b)
    part_b = [exchange_set(which, units_b, choice, dev_count) for which in range(3)]

    coarse_features = merge_features(collect(units_x, part_x), src).T
    coarse_adjacency = merge_tiles(collect(units_a, part_a), src, 0, None)
    coarse_adjacency = merge_tiles(collect(units_b, part_b), src, rows, coarse_adjacency)
    return coarse_adjacency, coarse_features


def solution(mesh):
    in_specs = (
        P("dev", "grp", None),
        P("dev", "grp"),
        P("dev", None),
        P("grp", None),
        P(),
        P(),
        P(),
    )
    out_specs = (P("dev", "grp", None), P("dev", "grp"))
    return jax.shard_map(body, mesh=mesh, in_specs=in_specs, out_specs=out_specs, check_vma=False)
```

time: 238 us -> 157 us (0.66)
  waiting for transfers between devices: 129 us -> 78.8 us
  loops' own time: 28.5 us -> 0.3 us
  starting transfers between devices: 16.4 us -> 26.8 us
  local copies, waits for them, and re-layouts: 23.6 us -> 14.7 us
  between operations: 5.32 us -> 2.94 us
    ppermute x15 -> x12, waiting for transfers between devices: 99 us -> 58.6 us  [turn(): lax.ppermute(x, 'dev', [(i, (i + shift) % dev_count) for i in range(dev_c...]
    another operation x21 -> x9, loops' own time: 28.5 us -> 0.3 us  [exchange_set(): lax.switch(choice[which], [branch(c) for c in range(3 ** len(shifts))], *...]
    ppermute x15 -> x12, starting transfers between devices: 5.73 us -> 16.9 us  [turn(): lax.ppermute(x, 'dev', [(i, (i + shift) % dev_count) for i in range(dev_c...]
    dynamic_slice x15 -> x0, local copies, waits for them, and re-layouts: 9.61 us -> none  [run(): piece = lax.dynamic_slice(blocks, (start, 0, 0), (size,) + rest)]
    ppermute x8, waiting for transfers between devices: 29.8 us -> 20.2 us  [the longest x2 19 us: second_step(): lax.ppermute(sums[0], 'grp', y_side)]
    unnamed x28 -> x46, local copies, waits for them, and re-layouts: 4.56 us -> 14 us
    another operation x6 -> x0, local copies, waits for them, and re-layouts: 4.34 us -> none
    concatenate x6 -> x0, local copies, waits for them, and re-layouts: 4.34 us -> none  [run(): jnp.concatenate([got, jnp.zeros((capacity - size,) + rest, jnp.float32)])]
  transfers between devices with their start and end apart: 23 -> 20, of which waited for: 17 -> 15; matrix products, arithmetic and copies ran while one was open for 7% -> 1% of each run, Pallas kernels for 6% -> 9%
where the time goes in v2:
time: 157 us; the launch traced here: 158 us
  waiting for transfers between devices  78.8 us (50%)
  Pallas kernels  28.5 us (18%)
  starting transfers between devices  26.8 us (17%)
  local copies, waits for them, and re-layouts  14.7 us (9%)
  other arithmetic  5.93 us (4%)
  between operations  2.94 us (2%)
    ppermute x12, waiting for transfers between devices, turn(): lax.ppermute(x, 'dev', [(i, (i + shift) % dev_count) for i in range(dev_c...  58.6 us
    ppermute x2, waiting for transfers between devices, second_step(): lax.ppermute(sums[0], 'grp', y_side)  19 us
    ppermute x12, starting transfers between devices, turn(): lax.ppermute(x, 'dev', [(i, (i + shift) % dev_count) for i in range(dev_c...  16.9 us
    unnamed x46, local copies, waits for them, and re-layouts  14 us
    pallas_call x2, Pallas kernels, column_map(): pl.pallas_call(functools.partial(columns_kernel, step_blocks, steps, full...  9.3 us
    pallas_call x2, Pallas kernels, row_map(): pl.pallas_call(functools.partial(rows_kernel, first, rows, step_blocks),...  6.55 us
    pallas_call x2, Pallas kernels, merge_tiles(): pl.pallas_call(functools.partial(merge_kernel, len(pieces), False), grid=...  6.45 us
    add x3, other arithmetic, partial_sums(): return (maps[1][1] + got[0][1], maps[3][1] + got[1][1])  5.33 us
  transfers between devices with their start and end apart: 20, of which 15 were waited for; matrix products, arithmetic and copies ran while one was open for 1% of the time, Pallas kernels for 9%

profile of v2, /device:TPU:0, one launch (start us, length us, event | category | flops | bytes accessed | tf_op | source)
XLA Modules:
  0.0 157.9 jit_solution(8842632888981781063)
XLA Ops:
  4.2 3.7 %row_map.3 = (f32[2,16,64,128]{3,2,1,0:T(8,128)}, f32[2,16,64,128]{3,2,1,0:T(8,128)S(1)}, f32[2,16,64,128]{3,2,1,0:T(8,128)}, f32[2,16,64,128]{3,2,1,0:T(8,128)S(1)}) custom-call(s32[8]{0:T(128)S(1)} %copy-done.16, s32[2,128]{1,0:T(2,128)S(1)} %copy-done.15, f32[32,256,128]{2,1,0:T(8,128)S(1)} %copy-done, f32[32,256,128]{2,1,0:T(8,128)S(1)} %copy-done, ...), custom_call_target="tpu_custom_call" | custom-call | flops 2000000000 | bytes 12582912 | tf_op jit(solution)/shard_map/row_map/pallas_call | solution.py:71
  7.9 2.9 %collective-permute-start.234 = (f32[2,16,64,128]{3,2,1,0:T(8,128)}, f32[2,16,64,128]{3,2,1,0:T(8,128)}, u32[]{:S(2)}, u32[]{:S(2)}) collective-permute-start(f32[2,16,64,128]{3,2,1,0:T(8,128)} %get-tuple-element.1259), channel_id=1, source_target_pairs={{0,8},{8,0},{16,24},{24,16},{1,9},{9,1},{17,25},{25,17},{2,10},{10... | collective-permute-start | bytes 3145736 | tf_op jit(solution)/shard_map/ppermute | solution.py:318
  12.6 3.0 %feature_map.1 = (f32[8,64,128]{2,1,0:T(8,128)S(1)}, f32[8,64,128]{2,1,0:T(8,128)}, f32[8,64,128]{2,1,0:T(8,128)}, f32[8,64,128]{2,1,0:T(8,128)S(1)}, f32[8,64,1...) custom-call(s32[32]{0:T(128)S(1)} %get-tuple-element.1466.slot_ref, ...), custom_call_target="tpu_custom_call" | custom-call | flops 1000000000 | bytes 2097152 | tf_op jit(solution)/shard_map/feature_map/pallas_call | solution.py:167
  16.3 2.8 %row_map.2 = (f32[2,16,64,128]{3,2,1,0:T(8,128)S(1)}, f32[2,16,64,128]{3,2,1,0:T(8,128)S(1)}, f32[2,16,64,128]{3,2,1,0:T(8,128)S(1)}, f32[2,16,64,128]{3,2,1,0:T(8,128)S(1)}) custom-call(s32[8]{0:T(128)S(1)} %copy-done.16, s32[2,128]{1,0:T(2,128)S(1)} %copy-done.15, f32[32,256,128]{2,1,0:T(8,128)S(1)} %copy-done.1, f32[32,256,128]{2,1,0:T(8,128)S(1)} %copy-done.1, ...), custom_call_target="tpu_custom_call" | custom-call | flops 2000000000 | bytes 12582912 | tf_op jit(solution)/shard_map/row_map/pallas_call | solution.py:71
  23.4 14.8 %conditional.10 = ((f32[8,64,128]{2,1,0:T(8,128)}, f32[4,64,128]{2,1,0:T(8,128)}, f32[8,64,128]{2,1,0:T(8,128)}, f32[4,64,128]{2,1,0:T(8,128)})) conditional(s32[]{:T(128)} %bitcast.2, () %tuple.570, f32[4,64,128]{2,1,0:T(8,128)} %get-tuple-element.1305, f32[8,64,128]{2,1,0:T(8,128)} %get-tuple-element.1306, ...), branch_computations={%region_32.33_spmd, %region_33.34_spmd, %region_34.35_spmd, %regio... | conditional | bytes 2097272 | solution.py:274
  27.3 7.6 %collective-permute-done.64 = f32[8,64,128]{2,1,0:T(8,128)} collective-permute-done((f32[8,64,128]{2,1,0:T(8,128)}, f32[8,64,128]{2,1,0:T(8,128)}, u32[]{:S(2)}, u32[]{:S(2)}) %collective-permute-start.64) | collective-permute-done | bytes 262176 | tf_op jit(solution)/shard_map/cond/branch_8_fun/ppermute | solution.py:243
  34.9 3.3 %collective-permute-done.65 = f32[8,64,128]{2,1,0:T(8,128)} collective-permute-done((f32[8,64,128]{2,1,0:T(8,128)}, f32[8,64,128]{2,1,0:T(8,128)}, u32[]{:S(2)}, u32[]{:S(2)}) %collective-permute-start.65) | collective-permute-done | bytes 262176 | tf_op jit(solution)/shard_map/cond/branch_8_fun/ppermute | solution.py:243
  38.2 11.5 %conditional.9 = ((f32[8,64,128]{2,1,0:T(8,128)}, f32[4,64,128]{2,1,0:T(8,128)}, f32[8,64,128]{2,1,0:T(8,128)}, f32[4,64,128]{2,1,0:T(8,128)}, f32[8,64,128]{2,1,0:T(8,128)}, /*index=5*/f32[4,64,128]{2,1,0:T(8,128)})) conditional(s32[]{:T(128)} %bitcast, () %tuple.547, ...), branch_computations={%region_5.6_spmd, %region_6.7_spmd, %region_7.8_spmd, %region_8.9_... | conditional | bytes 3145904 | solution.py:274
  39.6 6.4 %collective-permute-done.3 = f32[4,64,128]{2,1,0:T(8,128)} collective-permute-done((f32[4,64,128]{2,1,0:T(8,128)}, f32[4,64,128]{2,1,0:T(8,128)}, u32[]{:S(2)}, u32[]{:S(2)}) %collective-permute-start.3) | collective-permute-done | bytes 131104 | tf_op jit(solution)/shard_map/cond/branch_4_fun/ppermute | solution.py:243
  45.9 3.8 %collective-permute-done.4 = f32[4,64,128]{2,1,0:T(8,128)} collective-permute-done((f32[4,64,128]{2,1,0:T(8,128)}, f32[4,64,128]{2,1,0:T(8,128)}, u32[]{:S(2)}, u32[]{:S(2)}) %collective-permute-start.4) | collective-permute-done | bytes 131104 | tf_op jit(solution)/shard_map/cond/branch_4_fun/ppermute | solution.py:243
  49.7 2.5 %add_bitcast_fusion.2 = (f32[16,64,128]{2,1,0:T(8,128)}, f32[16,64,128]{2,1,0:T(8,128)}) fusion(f32[2,16,64,128]{3,2,1,0:T(8,128)} %collective-permute-done.235.refs_4_, f32[2,16,64,128]{3,2,1,0:T(8,128)} %copy-done.4, f32[2,16,64,128]{3,2,1,0:T(8,128)} %collective-permute-done.234.refs_1_, f32[2,16,64,128]{3,2,1,0:T(8,128)S(1)} %get-tuple-element.1327.refs_0_), kind=kLoop, calls=%fused_computation.2 | loop fusion | flops 262144 | bytes 3145728 | tf_op jit(solution)/shard_map/add | solution.py:321
  54.0 12.4 %collective-permute-done.236.refs_2_ = f32[16,64,128]{2,1,0:T(8,128)S(1)} collective-permute-done((f32[16,64,128]{2,1,0:T(8,128)}, f32[16,64,128]{2,1,0:T(8,128)S(1)}, u32[]{:S(2)}, u32[]{:S(2)}) %collective-permute-start.236) | collective-permute-done | bytes 524320 | tf_op jit(solution)/shard_map/ppermute | solution.py:324
  74.1 4.6 %column_map.2 = (f32[8,64,128]{2,1,0:T(8,128)S(1)}, f32[8,64,128]{2,1,0:T(8,128)}, f32[8,64,128]{2,1,0:T(8,128)}, f32[8,64,128]{2,1,0:T(8,128)}, f32[8,64,128]{2...) custom-call(s32[32]{0:T(128)S(1)} %get-tuple-element.1466.slot_ref, ...), custom_call_target="tpu_custom_call" | custom-call | flops 1000000000 | bytes 4194304 | tf_op jit(solution)/shard_map/column_map/pallas_call | solution.py:153
  78.7 12.7 %conditional.13 = ((f32[8,64,128]{2,1,0:T(8,128)}, f32[4,64,128]{2,1,0:T(8,128)}, f32[8,64,128]{2,1,0:T(8,128)}, f32[4,64,128]{2,1,0:T(8,128)})) conditional(s32[]{:T(128)} %bitcast.2, () %tuple.604, f32[4,64,128]{2,1,0:T(8,128)} %get-tuple-element.1365, f32[8,64,128]{2,1,0:T(8,128)} %get-tuple-element.1366, ...), branch_computations={%region_77.78_spmd, %region_78.79_spmd, %region_79.80_spmd, %regio... | conditional | bytes 2097272 | solution.py:274
  78.8 3.8 %collective-permute-start.143 = (f32[8,64,128]{2,1,0:T(8,128)}, f32[8,64,128]{2,1,0:T(8,128)}, u32[]{:S(2)}, u32[]{:S(2)}) collective-permute-start(f32[8,64,128]{2,1,0:T(8,128)} %get-tuple-element.808), channel_id=1, source_target_pairs={{0,6},{1,7},{2,0},{3,1},{4,2},{5,3},{6,4},{7,5},{8,14},{9,15},{10,... | collective-permute-start | bytes 786440 | tf_op jit(solution)/shard_map/cond/branch_8_fun/ppermute | solution.py:243
  82.6 7.5 %collective-permute-done.142 = f32[8,64,128]{2,1,0:T(8,128)} collective-permute-done((f32[8,64,128]{2,1,0:T(8,128)}, f32[8,64,128]{2,1,0:T(8,128)}, u32[]{:S(2)}, u32[]{:S(2)}) %collective-permute-start.142) | collective-permute-done | bytes 262176 | tf_op jit(solution)/shard_map/cond/branch_8_fun/ppermute | solution.py:243
  91.4 11.4 %conditional.12 = ((f32[8,64,128]{2,1,0:T(8,128)}, f32[4,64,128]{2,1,0:T(8,128)}, f32[8,64,128]{2,1,0:T(8,128)}, f32[4,64,128]{2,1,0:T(8,128)}, f32[8,64,128]{2,1,0:T(8,128)}, /*index=5*/f32[4,64,128]{2,1,0:T(8,128)})) conditional(s32[]{:T(128)} %bitcast, () %tuple.583, ...), branch_computations={%region_50.51_spmd, %region_51.52_spmd, %region_52.53_spmd, %regio... | conditional | bytes 3145904 | solution.py:274
  91.4 2.3 %collective-permute-start.82 = (f32[4,64,128]{2,1,0:T(8,128)}, f32[4,64,128]{2,1,0:T(8,128)}, u32[]{:S(2)}, u32[]{:S(2)}) collective-permute-start(f32[4,64,128]{2,1,0:T(8,128)} %get-tuple-element.650), channel_id=1, source_target_pairs={{0,4},{1,5},{2,6},{3,7},{4,0},{5,1},{6,2},{7,3},{8,12},{9,13},{10,... | collective-permute-start | bytes 393224 | tf_op jit(solution)/shard_map/cond/branch_4_fun/ppermute | solution.py:243
  93.7 5.2 %collective-permute-done.81 = f32[4,64,128]{2,1,0:T(8,128)} collective-permute-done((f32[4,64,128]{2,1,0:T(8,128)}, f32[4,64,128]{2,1,0:T(8,128)}, u32[]{:S(2)}, u32[]{:S(2)}) %collective-permute-start.81) | collective-permute-done | bytes 131104 | tf_op jit(solution)/shard_map/cond/branch_4_fun/ppermute | solution.py:243
  98.9 3.8 %collective-permute-done.82 = f32[4,64,128]{2,1,0:T(8,128)} collective-permute-done((f32[4,64,128]{2,1,0:T(8,128)}, f32[4,64,128]{2,1,0:T(8,128)}, u32[]{:S(2)}, u32[]{:S(2)}) %collective-permute-start.82) | collective-permute-done | bytes 131104 | tf_op jit(solution)/shard_map/cond/branch_4_fun/ppermute | solution.py:243
  109.5 3.2 %merge_features.1 = f32[64,2048]{1,0:T(8,128)} custom-call(s32[32]{0:T(128)S(1)} %select_reduce_fusion.src_ref, f32[8,64,128]{2,1,0:T(8,128)S(1)} %copy-done.11, f32[8,64,128]{2,1,0:T(8,128)} %get-tuple-element.1450.refs_1_, f32[8,64,128]{2,1,0:T(8,128)} %get-tuple-element.1451.refs_2_, f32[8,64,128]{2,1,0:T(8,128)} %get-tuple-element.1452.refs_3_, ...), custom_call_target="tpu_custom_call" | custom-call | flops 1000000 | bytes 3145728 | tf_op jit(solution)/shard_map/merge_features/pallas_call | solution.py:209
  112.8 6.6 %collective-permute-done.240.refs_2_ = f32[16,64,128]{2,1,0:T(8,128)} collective-permute-done((f32[16,64,128]{2,1,0:T(8,128)}, f32[16,64,128]{2,1,0:T(8,128)}, u32[]{:S(2)}, u32[]{:S(2)}) %collective-permute-start.240) | collective-permute-done | bytes 524320 | tf_op jit(solution)/shard_map/ppermute | solution.py:324
  120.6 4.7 %column_map.3 = (f32[8,64,128]{2,1,0:T(8,128)S(1)}, f32[8,64,128]{2,1,0:T(8,128)}, f32[8,64,128]{2,1,0:T(8,128)}, f32[8,64,128]{2,1,0:T(8,128)}, f32[8,64,128]{2...) custom-call(s32[32]{0:T(128)S(1)} %get-tuple-element.1466.slot_ref, ...), custom_call_target="tpu_custom_call" | custom-call | flops 1000000000 | bytes 4194304 | tf_op jit(solution)/shard_map/column_map/pallas_call | solution.py:153
  126.0 13.6 %conditional.16 = ((f32[8,64,128]{2,1,0:T(8,128)}, f32[4,64,128]{2,1,0:T(8,128)}, f32[8,64,128]{2,1,0:T(8,128)}, f32[4,64,128]{2,1,0:T(8,128)})) conditional(s32[]{:T(128)} %bitcast.2, () %tuple.638, f32[4,64,128]{2,1,0:T(8,128)} %get-tuple-element.1413, f32[8,64,128]{2,1,0:T(8,128)} %get-tuple-element.1414, ...), branch_computations={%region_122.123_spmd, %region_123.124_spmd, %region_124.125_spmd, ... | conditional | bytes 2097272 | solution.py:274
  126.0 3.8 %collective-permute-start.221 = (f32[8,64,128]{2,1,0:T(8,128)}, f32[8,64,128]{2,1,0:T(8,128)}, u32[]{:S(2)}, u32[]{:S(2)}) collective-permute-start(f32[8,64,128]{2,1,0:T(8,128)} %get-tuple-element.1014), channel_id=1, source_target_pairs={{0,6},{1,7},{2,0},{3,1},{4,2},{5,3},{6,4},{7,5},{8,14},{9,15},{10,... | collective-permute-start | bytes 786440 | tf_op jit(solution)/shard_map/cond/branch_8_fun/ppermute | solution.py:243
  129.8 7.5 %collective-permute-done.220 = f32[8,64,128]{2,1,0:T(8,128)} collective-permute-done((f32[8,64,128]{2,1,0:T(8,128)}, f32[8,64,128]{2,1,0:T(8,128)}, u32[]{:S(2)}, u32[]{:S(2)}) %collective-permute-start.220) | collective-permute-done | bytes 262176 | tf_op jit(solution)/shard_map/cond/branch_8_fun/ppermute | solution.py:243
  137.4 2.3 %collective-permute-done.221 = f32[8,64,128]{2,1,0:T(8,128)} collective-permute-done((f32[8,64,128]{2,1,0:T(8,128)}, f32[8,64,128]{2,1,0:T(8,128)}, u32[]{:S(2)}, u32[]{:S(2)}) %collective-permute-start.221) | collective-permute-done | bytes 262176 | tf_op jit(solution)/shard_map/cond/branch_8_fun/ppermute | solution.py:243
  139.6 3.2 %merge_tiles.2.refs_15_ = f32[16,128,128]{2,1,0:T(8,128)} custom-call(s32[32]{0:T(128)S(1)} %select_reduce_fusion.src_ref, f32[8,64,128]{2,1,0:T(8,128)S(1)} %get-tuple-element.1434.refs_0_, f32[8,64,128]{2,1,0:T(8,128)} %get-tuple-element.1435.refs_1_, f32[8,64,128]{2,1,0:T(8,128)} %get-tuple-element.1436.refs_2_, ...), custom_call_target="tpu_custom_call" | custom-call | flops 1000000 | bytes 3145728 | tf_op jit(solution)/shard_map/merge_tiles/pallas_call | solution.py:225
  142.9 11.6 %conditional.15 = ((f32[8,64,128]{2,1,0:T(8,128)}, f32[4,64,128]{2,1,0:T(8,128)}, f32[8,64,128]{2,1,0:T(8,128)}, f32[4,64,128]{2,1,0:T(8,128)}, f32[8,64,128]{2,1,0:T(8,128)}, /*index=5*/f32[4,64,128]{2,1,0:T(8,128)})) conditional(s32[]{:T(128)} %bitcast, () %tuple.617, ...), branch_computations={%region_95.96_spmd, %region_96.97_spmd, %region_97.98_spmd, %regio... | conditional | bytes 3145904 | solution.py:274
  144.6 5.8 %collective-permute-done.159 = f32[4,64,128]{2,1,0:T(8,128)} collective-permute-done((f32[4,64,128]{2,1,0:T(8,128)}, f32[4,64,128]{2,1,0:T(8,128)}, u32[]{:S(2)}, u32[]{:S(2)}) %collective-permute-start.159) | collective-permute-done | bytes 131104 | tf_op jit(solution)/shard_map/cond/branch_4_fun/ppermute | solution.py:243
  150.4 4.1 %collective-permute-done.160 = f32[4,64,128]{2,1,0:T(8,128)} collective-permute-done((f32[4,64,128]{2,1,0:T(8,128)}, f32[4,64,128]{2,1,0:T(8,128)}, u32[]{:S(2)}, u32[]{:S(2)}) %collective-permute-start.160) | collective-permute-done | bytes 131104 | tf_op jit(solution)/shard_map/cond/branch_4_fun/ppermute | solution.py:243
  154.5 3.2 %merge_tiles.3 = f32[16,128,128]{2,1,0:T(8,128)} custom-call(s32[32]{0:T(128)S(1)} %select_reduce_fusion.src_ref, f32[8,64,128]{2,1,0:T(8,128)S(1)} %copy-done.13, f32[8,64,128]{2,1,0:T(8,128)} %get-tuple-element.1412.refs_1_, f32[8,64,128]{2,1,0:T(8,128)} %get-tuple-element.1417.refs_2_, ...), custom_call_target="tpu_custom_call", output_to_operand_aliasing={{}: (16, {})} | custom-call | flops 1000000 | bytes 3145728 | tf_op jit(solution)/shard_map/merge_tiles/pallas_call | solution.py:225
  (90 shorter events, 34.4 us)
Async XLA Ops:
  0.6 2.2 %copy-start = (f32[32,256,128]{2,1,0:T(8,128)S(1)}, f32[32,256,128]{2,1,0:T(8,128)}, u32[]{:S(2)}) copy-start(f32[32,256,128]{2,1,0:T(8,128)} %refs_7_.3) | copy-start | bytes 12582916
  4.2 8.2 %copy-start.20 = (s32[32]{0:T(128)S(1)}, s32[32]{0:T(128)}, u32[]{:S(2)}) copy-start(s32[32]{0:T(128)} %param.149) | copy-start | bytes 388
  4.2 8.4 %copy-start.14 = (s32[32,128]{1,0:T(8,128)S(1)}, s32[32,128]{1,0:T(8,128)}, u32[]{:S(2)}) copy-start(s32[32,128]{1,0:T(8,128)} %col_ref.5) | copy-start | bytes 49156
  4.2 8.4 %copy-start.17 = (f32[4096,64]{0,1:T(8,128)S(1)}, f32[4096,64]{0,1:T(8,128)}, u32[]{:S(2)}) copy-start(f32[4096,64]{0,1:T(8,128)} %param.144) | copy-start | bytes 3145732
  4.2 12.1 %copy-start.1 = (f32[32,256,128]{2,1,0:T(8,128)S(1)}, f32[32,256,128]{2,1,0:T(8,128)}, u32[]{:S(2)}) copy-start(f32[32,256,128]{2,1,0:T(8,128)} %refs_7_.3) | copy-start | bytes 12582916
  7.9 11.2 %copy-start.4 = (f32[2,16,64,128]{3,2,1,0:T(8,128)}, f32[2,16,64,128]{3,2,1,0:T(8,128)S(1)}, u32[]{:S(2)}) copy-start(f32[2,16,64,128]{3,2,1,0:T(8,128)S(1)} %get-tuple-element.1329.refs_3_) | copy-start | bytes 3145732
  7.9 41.8 %copy-start.2 = (f32[2,16,64,128]{3,2,1,0:T(8,128)}, f32[2,16,64,128]{3,2,1,0:T(8,128)S(1)}, u32[]{:S(2)}) copy-start(f32[2,16,64,128]{3,2,1,0:T(8,128)S(1)} %get-tuple-element.1327.refs_0_) | copy-start | bytes 3145732
  7.9 41.8 %collective-permute-start.234 = (f32[2,16,64,128]{3,2,1,0:T(8,128)}, f32[2,16,64,128]{3,2,1,0:T(8,128)}, u32[]{:S(2)}, u32[]{:S(2)}) collective-permute-start(f32[2,16,64,128]{3,2,1,0:T(8,128)} %get-tuple-element.1259), channel_id=1, source_target_pairs={{0,8},{8,0},{16,24},{24,16},{1,9},{9,1},{17,25},{25,17},{2,10},{10... | collective-permute-start | bytes 3145736 | tf_op jit(solution)/shard_map/ppermute | solution.py:318
  10.8 38.9 %collective-permute-start.235 = (f32[2,16,64,128]{3,2,1,0:T(8,128)}, f32[2,16,64,128]{3,2,1,0:T(8,128)}, u32[]{:S(2)}, u32[]{:S(2)}) collective-permute-start(f32[2,16,64,128]{3,2,1,0:T(8,128)} %get-tuple-element.1261), channel_id=1, source_target_pairs={{0,16},{8,24},{16,0},{24,8},{1,17},{9,25},{17,1},{25,9},{2,18},{10... | collective-permute-start | bytes 3145736 | tf_op jit(solution)/shard_map/ppermute | solution.py:318
  16.3 5.0 %copy-start.21 = (s32[3,8]{1,0:T(4,128)S(1)}, s32[3,8]{1,0:T(4,128)}, u32[]{:S(2)}) copy-start(s32[3,8]{1,0:T(4,128)} %constant.27.clone) | copy-start | bytes 292
  23.4 11.5 %collective-permute-start.64 = (f32[8,64,128]{2,1,0:T(8,128)}, f32[8,64,128]{2,1,0:T(8,128)}, u32[]{:S(2)}, u32[]{:S(2)}) collective-permute-start(f32[8,64,128]{2,1,0:T(8,128)} %get-tuple-element.600), channel_id=1, source_target_pairs={{0,2},{1,3},{2,4},{3,5},{4,6},{5,7},{6,0},{7,1},{8,10},{9,11},{10,... | collective-permute-start | bytes 786440 | tf_op jit(solution)/shard_map/cond/branch_8_fun/ppermute | solution.py:243
  25.1 13.1 %collective-permute-start.65 = (f32[8,64,128]{2,1,0:T(8,128)}, f32[8,64,128]{2,1,0:T(8,128)}, u32[]{:S(2)}, u32[]{:S(2)}) collective-permute-start(f32[8,64,128]{2,1,0:T(8,128)} %get-tuple-element.602), channel_id=1, source_target_pairs={{0,6},{1,7},{2,0},{3,1},{4,2},{5,3},{6,4},{7,5},{8,14},{9,15},{10,... | collective-permute-start | bytes 786440 | tf_op jit(solution)/shard_map/cond/branch_8_fun/ppermute | solution.py:243
  38.2 7.8 %collective-permute-start.3 = (f32[4,64,128]{2,1,0:T(8,128)}, f32[4,64,128]{2,1,0:T(8,128)}, u32[]{:S(2)}, u32[]{:S(2)}) collective-permute-start(f32[4,64,128]{2,1,0:T(8,128)} %get-tuple-element.442), channel_id=1, source_target_pairs={{0,1},{1,2},{2,3},{3,4},{4,5},{5,6},{6,7},{7,0},{8,9},{9,10},{10,1... | collective-permute-start | bytes 393224 | tf_op jit(solution)/shard_map/cond/branch_4_fun/ppermute | solution.py:243
  38.2 11.5 %collective-permute-start.4 = (f32[4,64,128]{2,1,0:T(8,128)}, f32[4,64,128]{2,1,0:T(8,128)}, u32[]{:S(2)}, u32[]{:S(2)}) collective-permute-start(f32[4,64,128]{2,1,0:T(8,128)} %get-tuple-element.444), channel_id=1, source_target_pairs={{0,4},{1,5},{2,6},{3,7},{4,0},{5,1},{6,2},{7,3},{8,12},{9,13},{10,... | collective-permute-start | bytes 393224 | tf_op jit(solution)/shard_map/cond/branch_4_fun/ppermute | solution.py:243
  52.3 14.2 %collective-permute-start.236 = (f32[16,64,128]{2,1,0:T(8,128)}, f32[16,64,128]{2,1,0:T(8,128)S(1)}, u32[]{:S(2)}, u32[]{:S(2)}) collective-permute-start(f32[16,64,128]{2,1,0:T(8,128)} %get-tuple-element.1348), channel_id=1, source_target_pairs={{0,16},{8,24},{16,0},{24,8},{1,17},{9,25},{17,1},{25,9},{2,18},{10... | collective-permute-start | bytes 1572872 | tf_op jit(solution)/shard_map/ppermute | solution.py:324
  52.8 14.4 %collective-permute-start.237 = (f32[16,64,128]{2,1,0:T(8,128)}, f32[16,64,128]{2,1,0:T(8,128)S(1)}, u32[]{:S(2)}, u32[]{:S(2)}) collective-permute-start(f32[16,64,128]{2,1,0:T(8,128)} %get-tuple-element.1349), channel_id=1, source_target_pairs={{0,8},{8,0},{16,24},{24,16},{1,9},{9,1},{17,25},{25,17},{2,10},{10... | collective-permute-start | bytes 1572872 | tf_op jit(solution)/shard_map/ppermute | solution.py:324
  68.0 34.8 %collective-permute-start.238 = (f32[2,16,64,128]{3,2,1,0:T(8,128)}, f32[2,16,64,128]{3,2,1,0:T(8,128)S(1)}, u32[]{:S(2)}, u32[]{:S(2)}) collective-permute-start(f32[2,16,64,128]{3,2,1,0:T(8,128)} %copy-done.19), channel_id=1, source_target_pairs={{0,8},{8,0},{16,24},{24,16},{1,9},{9,1},{17,25},{25,17},{2,10},{10... | collective-permute-start | bytes 3145736 | tf_op jit(solution)/shard_map/ppermute | solution.py:318
  68.5 34.2 %collective-permute-start.239 = (f32[2,16,64,128]{3,2,1,0:T(8,128)}, f32[2,16,64,128]{3,2,1,0:T(8,128)}, u32[]{:S(2)}, u32[]{:S(2)}) collective-permute-start(f32[2,16,64,128]{3,2,1,0:T(8,128)} %copy-done.18), channel_id=1, source_target_pairs={{0,16},{8,24},{16,0},{24,8},{1,17},{9,25},{17,1},{25,9},{2,18},{10... | collective-permute-start | bytes 3145736 | tf_op jit(solution)/shard_map/ppermute | solution.py:318
  69.5 1.2 copy-start.3
  70.7 1.2 copy-start.5
  74.1 34.4 %copy-start.22 = (s32[32]{0:T(128)S(1)}, s32[32]{0:T(128)}, u32[]{:S(2)}) copy-start(s32[32]{0:T(128)} %param.148) | copy-start | bytes 388
  78.7 11.4 %collective-permute-start.142 = (f32[8,64,128]{2,1,0:T(8,128)}, f32[8,64,128]{2,1,0:T(8,128)}, u32[]{:S(2)}, u32[]{:S(2)}) collective-permute-start(f32[8,64,128]{2,1,0:T(8,128)} %get-tuple-element.806), channel_id=1, source_target_pairs={{0,2},{1,3},{2,4},{3,5},{4,6},{5,7},{6,0},{7,1},{8,10},{9,11},{10,... | collective-permute-start | bytes 786440 | tf_op jit(solution)/shard_map/cond/branch_8_fun/ppermute | solution.py:243
  78.8 12.6 %collective-permute-start.143 = (f32[8,64,128]{2,1,0:T(8,128)}, f32[8,64,128]{2,1,0:T(8,128)}, u32[]{:S(2)}, u32[]{:S(2)}) collective-permute-start(f32[8,64,128]{2,1,0:T(8,128)} %get-tuple-element.808), channel_id=1, source_target_pairs={{0,6},{1,7},{2,0},{3,1},{4,2},{5,3},{6,4},{7,5},{8,14},{9,15},{10,... | collective-permute-start | bytes 786440 | tf_op jit(solution)/shard_map/cond/branch_8_fun/ppermute | solution.py:243
  91.4 7.6 %collective-permute-start.81 = (f32[4,64,128]{2,1,0:T(8,128)}, f32[4,64,128]{2,1,0:T(8,128)}, u32[]{:S(2)}, u32[]{:S(2)}) collective-permute-start(f32[4,64,128]{2,1,0:T(8,128)} %get-tuple-element.648), channel_id=1, source_target_pairs={{0,1},{1,2},{2,3},{3,4},{4,5},{5,6},{6,7},{7,0},{8,9},{9,10},{10,1... | collective-permute-start | bytes 393224 | tf_op jit(solution)/shard_map/cond/branch_4_fun/ppermute | solution.py:243
  91.4 11.4 %collective-permute-start.82 = (f32[4,64,128]{2,1,0:T(8,128)}, f32[4,64,128]{2,1,0:T(8,128)}, u32[]{:S(2)}, u32[]{:S(2)}) collective-permute-start(f32[4,64,128]{2,1,0:T(8,128)} %get-tuple-element.650), channel_id=1, source_target_pairs={{0,4},{1,5},{2,6},{3,7},{4,0},{5,1},{6,2},{7,3},{8,12},{9,13},{10,... | collective-permute-start | bytes 393224 | tf_op jit(solution)/shard_map/cond/branch_4_fun/ppermute | solution.py:243
  105.5 13.9 %collective-permute-start.240 = (f32[16,64,128]{2,1,0:T(8,128)}, f32[16,64,128]{2,1,0:T(8,128)}, u32[]{:S(2)}, u32[]{:S(2)}) collective-permute-start(f32[16,64,128]{2,1,0:T(8,128)} %add_bitcast_fusion.1), channel_id=1, source_target_pairs={{0,16},{8,24},{16,0},{24,8},{1,17},{9,25},{17,1},{25,9},{2,18},{10... | collective-permute-start | bytes 1572872 | tf_op jit(solution)/shard_map/ppermute | solution.py:324
  106.9 13.7 %collective-permute-start.241 = (f32[16,64,128]{2,1,0:T(8,128)}, f32[16,64,128]{2,1,0:T(8,128)}, u32[]{:S(2)}, u32[]{:S(2)}) collective-permute-start(f32[16,64,128]{2,1,0:T(8,128)} %add_bitcast_fusion), channel_id=1, source_target_pairs={{0,8},{8,0},{16,24},{24,16},{1,9},{9,1},{17,25},{25,17},{2,10},{10... | collective-permute-start | bytes 1572872 | tf_op jit(solution)/shard_map/ppermute | solution.py:324
  126.0 28.5 %copy-start.13 = (f32[8,64,128]{2,1,0:T(8,128)S(1)}, f32[8,64,128]{2,1,0:T(8,128)}, u32[]{:S(2)}) copy-start(f32[8,64,128]{2,1,0:T(8,128)} %copy-done.12) | copy-start | bytes 786436
  126.0 11.4 %collective-permute-start.220 = (f32[8,64,128]{2,1,0:T(8,128)}, f32[8,64,128]{2,1,0:T(8,128)}, u32[]{:S(2)}, u32[]{:S(2)}) collective-permute-start(f32[8,64,128]{2,1,0:T(8,128)} %get-tuple-element.1012), channel_id=1, source_target_pairs={{0,2},{1,3},{2,4},{3,5},{4,6},{5,7},{6,0},{7,1},{8,10},{9,11},{10,... | collective-permute-start | bytes 786440 | tf_op jit(solution)/shard_map/cond/branch_8_fun/ppermute | solution.py:243
  126.0 13.6 %collective-permute-start.221 = (f32[8,64,128]{2,1,0:T(8,128)}, f32[8,64,128]{2,1,0:T(8,128)}, u32[]{:S(2)}, u32[]{:S(2)}) collective-permute-start(f32[8,64,128]{2,1,0:T(8,128)} %get-tuple-element.1014), channel_id=1, source_target_pairs={{0,6},{1,7},{2,0},{3,1},{4,2},{5,3},{6,4},{7,5},{8,14},{9,15},{10,... | collective-permute-start | bytes 786440 | tf_op jit(solution)/shard_map/cond/branch_8_fun/ppermute | solution.py:243
  142.9 7.4 %collective-permute-start.159 = (f32[4,64,128]{2,1,0:T(8,128)}, f32[4,64,128]{2,1,0:T(8,128)}, u32[]{:S(2)}, u32[]{:S(2)}) collective-permute-start(f32[4,64,128]{2,1,0:T(8,128)} %get-tuple-element.854), channel_id=1, source_target_pairs={{0,1},{1,2},{2,3},{3,4},{4,5},{5,6},{6,7},{7,0},{8,9},{9,10},{10,1... | collective-permute-start | bytes 393224 | tf_op jit(solution)/shard_map/cond/branch_4_fun/ppermute | solution.py:243
  143.0 11.5 %collective-permute-start.160 = (f32[4,64,128]{2,1,0:T(8,128)}, f32[4,64,128]{2,1,0:T(8,128)}, u32[]{:S(2)}, u32[]{:S(2)}) collective-permute-start(f32[4,64,128]{2,1,0:T(8,128)} %get-tuple-element.856), channel_id=1, source_target_pairs={{0,4},{1,5},{2,6},{3,7},{4,0},{5,1},{6,2},{7,3},{8,12},{9,13},{10,... | collective-permute-start | bytes 393224 | tf_op jit(solution)/shard_map/cond/branch_4_fun/ppermute | solution.py:243
  (11 other events, 9.4 us)
